TPU v7x, 32 devices: a whole 2x2x4 slice. The times are simulated.
32 devices in a mesh: replica: 8 (over z, core), group: 4 (over y, x).
Axes of the slice: x: 2, y: 2, z: 4, core: 2. Of those that a mesh axis runs over, the one named last changes fastest.
Arguments:
- tokens: bfloat16 [4, 8192, 768], P('group', 'replica'), may hold values from -6 to 6
- cotangent: bfloat16 [4, 8192, 768], P('group', 'replica'), may hold values from -6 to 6
- lengths: int32 [4, 16], P('group'), may hold values from 256 to 768, as said below
- dealing: int32 [4, 16], P('group'), may hold values from 0 to 15, as said below
- offsets: int32 [4, 8, 2], P('group'), may hold values from 0 to 768, as said below
- attn_gain: float32 [768], P('group'), may hold values from 0.1 to 1.9
- qkv_weight: float32 [768, 2304], P('group'), may hold values from -0.21875 to 0.21875
- out_weight: float32 [768, 768], P('group'), may hold values from -0.875 to 0.875
- mlp_gain: float32 [768], P('group'), may hold values from 0.1 to 1.9
- in_weight: float32 [768, 2304], P('group'), may hold values from -0.21875 to 0.21875
- down_weight: float32 [1152, 768], P('group'), may hold values from -0.1875 to 0.1875
Outputs:
- output: bfloat16 [4, 8192, 768], P('group', 'replica')
- input_grad: bfloat16 [4, 8192, 768], P('group', 'replica')
- attn_gain_grad: float32 [768], P('group')
- qkv_grad: float32 [768, 2304], P('group')
- out_grad: float32 [768, 768], P('group')
- mlp_gain_grad: float32 [768], P('group')
- in_grad: float32 [768, 2304], P('group')
- down_grad: float32 [1152, 768], P('group')
Inputs may be any that keep to these rules, and one draw needn't show every extreme that they name: `lengths`: the 16 sequences of a column lie end to end over its 8192 tokens; the two sequences dealt to one replica index hold 1024 tokens together. `dealing`: for each column a permutation of its sequences: entry k is the given-order number of the sequence that is k-th in dealt order; replica index r takes dealt sequences 2 * r to 2 * r + 1. `offsets`: exclusive running sums of the lengths of each replica index's dealt sequences, in dealt order.
All inputs are finite; a program needn't handle non-finite values.
Results may differ from a plain program's by a relative error of at most 0.02.
Values may be sent and summed in bfloat16 or wider, within the bound.
No kernel may reach another device: no remote copies, remote signals or barrier semaphores. Data moves between devices by JAX's collectives and lax.ppermute only.
A program may use at most 256 MiB of HBM per device.

v0:
```python
import math

import jax
import jax.numpy as jnp
from jax import lax
from jax.sharding import PartitionSpec as P

HEADS = 12
HEAD_DIM = 64


epsilon = 1e-05
big_negative = -1e30
rope_base = 160000.0


def column_starts(lengths):
    return jnp.cumsum(lengths) - lengths


def dealt_map(lengths, dealing, offsets, replica_index, tok_rows):
    seq_count = lengths.shape[0]
    per_device = offsets.shape[1]
    starts = column_starts(lengths)
    slot_ids = jnp.arange(tok_rows, dtype=jnp.int32)
    own_starts = lax.dynamic_index_in_dim(offsets, replica_index, 0, keepdims=False)
    segment = jnp.sum((slot_ids[:, None] >= own_starts[None, 1:]).astype(jnp.int32), axis=1)
    choose = segment[:, None] == jnp.arange(per_device, dtype=jnp.int32)[None, :]
    begin_at = jnp.sum(jnp.where(choose, own_starts[None, :], 0), axis=1)
    positions = slot_ids - begin_at
    dealt = replica_index * per_device + segment
    seq_range = jnp.arange(seq_count, dtype=jnp.int32)
    dealt_hits = dealt[:, None] == seq_range[None, :]
    given = jnp.sum(jnp.where(dealt_hits, dealing[None, :], 0), axis=1)
    found_seq = given[:, None] == seq_range[None, :]
    first_at = jnp.sum(jnp.where(found_seq, starts[None, :], 0), axis=1)
    source = jnp.clip(first_at + positions, 0, tok_rows * offsets.shape[0] - 1)
    return (source, segment, positions)


def given_map(lengths, dealing, offsets, column_pos, tok_rows):
    seq_count = lengths.shape[0]
    per_device = offsets.shape[1]
    starts = column_starts(lengths)
    seq_range = jnp.arange(seq_count, dtype=jnp.int32)
    seq_id = jnp.sum((column_pos[:, None] >= starts[None, 1:]).astype(jnp.int32), axis=1)
    found_seq = seq_id[:, None] == seq_range[None, :]
    first_at = jnp.sum(jnp.where(found_seq, starts[None, :], 0), axis=1)
    positions = column_pos - first_at
    matches = dealing[None, :] == seq_id[:, None]
    dealt = jnp.sum(jnp.where(matches, seq_range[None, :], 0), axis=1)
    flat_starts = offsets.reshape(-1)
    dealt_hits = dealt[:, None] == seq_range[None, :]
    begin_at = jnp.sum(jnp.where(dealt_hits, flat_starts[None, :], 0), axis=1)
    target = dealt // per_device * tok_rows + begin_at + positions
    return jnp.clip(target, 0, tok_rows * offsets.shape[0] - 1)


def rotary(values, positions, head_count, head_dim):
    tok_rows = values.shape[0]
    half_dim = head_dim // 2
    frequency = jnp.exp(
        -(jnp.arange(half_dim, dtype=jnp.float32) * (2.0 / head_dim)) * math.log(rope_base)
    )
    angles = positions.astype(jnp.float32)[:, None] * frequency[None, :]
    cosine = jnp.cos(angles)[:, None, :]
    sine_part = jnp.sin(angles)[:, None, :]
    shaped = values.reshape(tok_rows, head_count, head_dim)
    lower_half = shaped[..., :half_dim]
    upper_half = shaped[..., half_dim:]
    turned = jnp.concatenate(
        [
            lower_half * cosine - upper_half * sine_part,
            upper_half * cosine + lower_half * sine_part,
        ],
        axis=-1,
    )
    return turned.reshape(tok_rows, head_count * head_dim)


def layer_norm(values, gain_vec):
    row_mean = jnp.mean(values, axis=-1, keepdims=True)
    centred = values - row_mean
    spread = jnp.mean(centred * centred, axis=-1, keepdims=True)
    return centred * lax.rsqrt(spread + epsilon) * gain_vec


def geglu(lifted):
    hidden_width = lifted.shape[1] // 2
    return jax.nn.gelu(lifted[:, :hidden_width], approximate=False) * lifted[:, hidden_width:]


def pick_rows(index_map, carry, piece):
    piece_rows = piece.shape[1]
    inside = (index_map >= 0) & (index_map < piece_rows)
    taken = jnp.take(piece[0], jnp.clip(index_map, 0, piece_rows - 1), axis=0)
    return jnp.where(inside[:, None], taken, carry)


def soft_block(queries, seg_query, key_heads, segment, score_scale):
    scores = (
        jnp.einsum("qhd,khd->hqk", queries, key_heads, preferred_element_type=jnp.float32)
        * score_scale
    )
    same_seq = seg_query[:, None] == segment[None, :]
    return jnp.where(same_seq[None], scores, big_negative)


def on_device(
    tokens,
    cotangent,
    lengths,
    dealing,
    offsets,
    attn_gain,
    qkv_weight,
    out_weight,
    mlp_gain,
    in_weight,
    down_weight,
):
    tok_rows = tokens.shape[1]
    model_width = tokens.shape[2]
    head_count = HEADS
    head_dim = HEAD_DIM
    score_scale = head_dim ** (-0.5)
    replica_index = lax.axis_index("replica")
    source, segment, positions = dealt_map(
        lengths[0], dealing[0], offsets[0], replica_index, tok_rows
    )
    target = given_map(
        lengths[0],
        dealing[0],
        offsets[0],
        replica_index * tok_rows + jnp.arange(tok_rows, dtype=jnp.int32),
        tok_rows,
    )
    masters = (
        attn_gain.astype(jnp.bfloat16),
        qkv_weight.astype(jnp.bfloat16),
        out_weight.astype(jnp.bfloat16),
        mlp_gain.astype(jnp.bfloat16),
        in_weight.astype(jnp.bfloat16),
        down_weight.astype(jnp.bfloat16),
    )
    weights = (
        lax.all_gather(masters[0], "group", axis=0, tiled=True),
        lax.all_gather(masters[1], "group", axis=0, tiled=True),
        lax.all_gather(masters[2], "group", axis=0, tiled=True),
        lax.all_gather(masters[3], "group", axis=0, tiled=True),
        lax.all_gather(masters[4], "group", axis=0, tiled=True),
        lax.all_gather(masters[5], "group", axis=0, tiled=True),
    )
    blank = jnp.zeros((tok_rows, model_width), jnp.bfloat16)
    dealt_x = pick_rows(source, blank, lax.all_gather(tokens, "replica", axis=1, tiled=True))
    gain_one, w_qkv, w_out, gain_two, w_in, w_down = weights
    gain_first = gain_one.astype(jnp.float32)
    gain_second = gain_two.astype(jnp.float32)
    rows_in = dealt_x.astype(jnp.float32)
    normed = layer_norm(rows_in, gain_first).astype(jnp.bfloat16)
    mixed_proj = jnp.dot(normed, w_qkv, preferred_element_type=jnp.float32)
    queries = (
        rotary(mixed_proj[:, :model_width], positions, head_count, head_dim)
        .astype(jnp.bfloat16)
        .reshape(tok_rows, head_count, head_dim)
    )
    key_heads = (
        rotary(mixed_proj[:, model_width : 2 * model_width], positions, head_count, head_dim)
        .astype(jnp.bfloat16)
        .reshape(tok_rows, head_count, head_dim)
    )
    value_heads = (
        mixed_proj[:, 2 * model_width :]
        .astype(jnp.bfloat16)
        .reshape(tok_rows, head_count, head_dim)
    )
    block_rows = min(512, tok_rows)
    block_count = tok_rows // block_rows
    attended_parts = []
    kept_tops = []
    kept_totals = []
    for number in range(block_count):
        lower_row = number * block_rows
        masked = soft_block(
            queries[lower_row : lower_row + block_rows],
            segment[lower_row : lower_row + block_rows],
            key_heads,
            segment,
            score_scale,
        )
        row_top = jnp.max(masked, axis=-1, keepdims=True)
        exponent = jnp.exp(masked - row_top)
        row_total = jnp.sum(exponent, axis=-1, keepdims=True)
        weights_soft = (exponent / row_total).astype(jnp.bfloat16)
        attended_block = jnp.einsum(
            "hqk,khd->qhd", weights_soft, value_heads, preferred_element_type=jnp.float32
        )
        attended_parts.append(attended_block.astype(jnp.bfloat16))
        kept_tops.append(row_top)
        kept_totals.append(row_total)
    attended = jnp.concatenate(attended_parts, axis=0).reshape(tok_rows, model_width)
    middle = rows_in + jnp.dot(attended, w_out, preferred_element_type=jnp.float32)
    normed_two = layer_norm(middle, gain_second).astype(jnp.bfloat16)
    lifted = jnp.dot(normed_two, w_in, preferred_element_type=jnp.float32)
    hidden = geglu(lifted).astype(jnp.bfloat16)
    output_dealt = (middle + jnp.dot(hidden, w_down, preferred_element_type=jnp.float32)).astype(
        jnp.bfloat16
    )
    output_given = pick_rows(
        target, blank, lax.all_gather(output_dealt[None], "replica", axis=1, tiled=True)
    )
    dealt_dy = pick_rows(source, blank, lax.all_gather(cotangent, "replica", axis=1, tiled=True))
    weights = (
        lax.all_gather(masters[0], "group", axis=0, tiled=True),
        lax.all_gather(masters[1], "group", axis=0, tiled=True),
        lax.all_gather(masters[2], "group", axis=0, tiled=True),
        lax.all_gather(masters[3], "group", axis=0, tiled=True),
        lax.all_gather(masters[4], "group", axis=0, tiled=True),
        lax.all_gather(masters[5], "group", axis=0, tiled=True),
    )
    gain_one, w_qkv, w_out, gain_two, w_in, w_down = weights
    grad_out = dealt_dy.astype(jnp.float32)
    down_partial = jnp.einsum("tf,td->fd", hidden, dealt_dy, preferred_element_type=jnp.float32)
    grad_hidden = jnp.einsum("td,fd->tf", dealt_dy, w_down, preferred_element_type=jnp.float32)
    _, geglu_back = jax.vjp(geglu, lifted)
    grad_lifted = geglu_back(grad_hidden)[0].astype(jnp.bfloat16)
    in_partial = jnp.einsum(
        "td,tf->df", normed_two, grad_lifted, preferred_element_type=jnp.float32
    )
    grad_normed_two = jnp.einsum("tf,df->td", grad_lifted, w_in, preferred_element_type=jnp.float32)
    _, norm_back_two = jax.vjp(layer_norm, middle, gain_second)
    grad_middle_part, gain_two_partial = norm_back_two(grad_normed_two)
    grad_middle = grad_out + grad_middle_part
    grad_branch = grad_middle.astype(jnp.bfloat16)
    out_partial = jnp.einsum("ti,to->io", attended, grad_branch, preferred_element_type=jnp.float32)
    grad_attended = (
        jnp.einsum("to,io->ti", grad_branch, w_out, preferred_element_type=jnp.float32)
        .astype(jnp.bfloat16)
        .reshape(tok_rows, head_count, head_dim)
    )
    grad_keys = jnp.zeros((tok_rows, head_count, head_dim), jnp.float32)
    grad_values = jnp.zeros((tok_rows, head_count, head_dim), jnp.float32)
    grad_query_parts = []
    for number in range(block_count):
        lower_row = number * block_rows
        query_block = queries[lower_row : lower_row + block_rows]
        masked = soft_block(
            query_block,
            segment[lower_row : lower_row + block_rows],
            key_heads,
            segment,
            score_scale,
        )
        weights_full = jnp.exp(masked - kept_tops[number]) / kept_totals[number]
        weights_soft = weights_full.astype(jnp.bfloat16)
        grad_block = grad_attended[lower_row : lower_row + block_rows]
        grad_probs = jnp.einsum(
            "qhd,khd->hqk", grad_block, value_heads, preferred_element_type=jnp.float32
        )
        inner = jnp.sum(weights_full * grad_probs, axis=-1, keepdims=True)
        grad_scores = (weights_full * (grad_probs - inner)).astype(jnp.bfloat16)
        grad_query_parts.append(
            jnp.einsum("hqk,khd->qhd", grad_scores, key_heads, preferred_element_type=jnp.float32)
            * score_scale
        )
        grad_keys = (
            grad_keys
            + jnp.einsum(
                "hqk,qhd->khd", grad_scores, query_block, preferred_element_type=jnp.float32
            )
            * score_scale
        )
        grad_values = grad_values + jnp.einsum(
            "hqk,qhd->khd", weights_soft, grad_block, preferred_element_type=jnp.float32
        )
    grad_queries = jnp.concatenate(grad_query_parts, axis=0).reshape(tok_rows, model_width)

    def turn_rows(values):
        return rotary(values, positions, head_count, head_dim)

    _, rope_back = jax.vjp(turn_rows, mixed_proj[:, :model_width])
    grad_mixed = jnp.concatenate(
        [
            rope_back(grad_queries)[0],
            rope_back(grad_keys.reshape(tok_rows, model_width))[0],
            grad_values.reshape(tok_rows, model_width),
        ],
        axis=1,
    ).astype(jnp.bfloat16)
    qkv_partial = jnp.einsum("td,te->de", normed, grad_mixed, preferred_element_type=jnp.float32)
    grad_normed = jnp.einsum("te,de->td", grad_mixed, w_qkv, preferred_element_type=jnp.float32)
    _, norm_back_one = jax.vjp(layer_norm, rows_in, gain_first)
    grad_rows_part, gain_one_partial = norm_back_one(grad_normed)
    grad_input = (grad_middle + grad_rows_part).astype(jnp.bfloat16)
    grad_given = pick_rows(
        target, blank, lax.all_gather(grad_input[None], "replica", axis=1, tiled=True)
    )
    partial_grads = (
        gain_one_partial,
        qkv_partial,
        out_partial,
        gain_two_partial,
        in_partial,
        down_partial,
    )
    shards = (
        lax.psum_scatter(
            partial_grads[0].astype(jnp.bfloat16), "group", scatter_dimension=0, tiled=True
        ).astype(jnp.float32),
        lax.psum_scatter(
            partial_grads[1].astype(jnp.bfloat16), "group", scatter_dimension=0, tiled=True
        ).astype(jnp.float32),
        lax.psum_scatter(
            partial_grads[2].astype(jnp.bfloat16), "group", scatter_dimension=0, tiled=True
        ).astype(jnp.float32),
        lax.psum_scatter(
            partial_grads[3].astype(jnp.bfloat16), "group", scatter_dimension=0, tiled=True
        ).astype(jnp.float32),
        lax.psum_scatter(
            partial_grads[4].astype(jnp.bfloat16), "group", scatter_dimension=0, tiled=True
        ).astype(jnp.float32),
        lax.psum_scatter(
            partial_grads[5].astype(jnp.bfloat16), "group", scatter_dimension=0, tiled=True
        ).astype(jnp.float32),
    )
    summed = (
        lax.psum(shards[0].astype(jnp.bfloat16), "replica").astype(jnp.float32),
        lax.psum(shards[1].astype(jnp.bfloat16), "replica").astype(jnp.float32),
        lax.psum(shards[2].astype(jnp.bfloat16), "replica").astype(jnp.float32),
        lax.psum(shards[3].astype(jnp.bfloat16), "replica").astype(jnp.float32),
        lax.psum(shards[4].astype(jnp.bfloat16), "replica").astype(jnp.float32),
        lax.psum(shards[5].astype(jnp.bfloat16), "replica").astype(jnp.float32),
    )
    return (
        output_given[None],
        grad_given[None],
        summed[0],
        summed[1],
        summed[2],
        summed[3],
        summed[4],
        summed[5],
    )


def solution(mesh):
    return jax.shard_map(
        on_device,
        mesh=mesh,
        in_specs=(
            P("group", "replica", None),
            P("group", "replica", None),
            P("group", None),
            P("group", None),
            P("group", None, None),
            P("group"),
            P("group", None),
            P("group", None),
            P("group"),
            P("group", None),
            P("group", None),
        ),
        out_specs=(
            P("group", "replica", None),
            P("group", "replica", None),
            P("group"),
            P("group", None),
            P("group", None),
            P("group"),
            P("group", None),
            P("group", None),
        ),
        check_vma=False,
    )
```

profile of v0, /device:TPU:0, one launch (start us, length us, event | category | flops | bytes accessed | tf_op | source)
XLA Modules:
  0.0 1020.1 jit_solution(18329896838933659207)
XLA Ops:
  21.5 11.3 %all-reduce.13 = (bf16[768]{0:T(1024)(128)(2,1)S(1)}, bf16[768]{0:T(1024)(128)(2,1)S(1)}) all-reduce(bf16[768]{0:T(1024)(128)(2,1)S(1)} %dynamic-update-slice, bf16[768]{0:T(1024)(128)(2,1)S(1)} %dynamic-update-slice.1), channel_id=1, replica_groups=mesh['replica'=8,'group'=4] {'group'}, use_global_device_ids=true, to_apply=%add.6 | all-reduce | flops 1536 | bytes 6144
  35.0 94.1 %all-gather.11.cloned.1.call-done = bf16[1,8192,768]{2,1,0:T(8,128)(2,1)} async-done(((bf16[1,1024,768]{2,1,0:T(8,128)(2,1)}), bf16[1,8192,768]{2,1,0:T(8,128)(2,1)}) %all-gather.11.cloned.1.call-update) | async-done | bytes 12582928 | tf_op jit(solution)/shard_map/all_gather | solution.py:155
  129.1 10.7 %gather_fusion = bf16[1024,768]{1,0:T(8,128)(2,1)S(1)} fusion(bf16[8192,768]{1,0:T(8,128)(2,1)} %bitcast.69, s32[1024]{0:T(1024)S(1)} %get-tuple-element.93), kind=kCustom, calls=%fused_computation.clone | custom fusion | bytes 3149824 | tf_op jit(solution)/shard_map/jit(_take)/gather | solution.py:96
  141.7 35.3 %all-gather.13.cloned.1.call-done = bf16[768,2304]{1,0:T(8,128)(2,1)} async-done(((bf16[192,2304]{1,0:T(8,128)(2,1)}), bf16[768,2304]{1,0:T(8,128)(2,1)}) %all-gather.13.cloned.1.call-update) | async-done | bytes 3538960 | tf_op jit(solution)/shard_map/all_gather | solution.py:148
  199.7 10.4 %fusion.62 = f32[12,512,1024]{2,1,0:T(8,128)} fusion(bf16[1024,12,32]{0,2,1:T(8,128)(2,1)S(1)} %get-tuple-element.82, bf16[1024,12,32]{0,2,1:T(8,128)(2,1)S(1)} %get-tuple-element.83, bf16[1024,12,32]{0,2,1:T(8,128)(2,1)S(1)} %get-tuple-element.75, bf16[1024,12,32]{0,2,1:T(8,128)(2,1)S(1)} %get-tuple-element.74), kind=kOutput, calls=%fused_computation.126 | convolution fusion | flops 810024960 | bytes 28311552 | tf_op jit(solution)/shard_map/qhd,khd->hqk/dot_general | solution.py:102
  210.2 14.6 %fusion.109 = (f32[12,512]{1,0:T(8,128)S(1)}, f32[12,512,1024]{2,1,0:T(8,128)}) fusion(pred[512,1024]{1,0:T(8,128)(4,1)} %get-tuple-element.88, bf16[1024,12,32]{0,2,1:T(8,128)(2,1)} %copy-done.17, bf16[1024,12,32]{0,2,1:T(8,128)(2,1)} %copy-done.15, bf16[1024,12,32]{0,2,1:T(8,128)(2,1)S(1)} %get-tuple-element.83, ...), kind=kOutput, calls=%fused_computation.205 | convolution fusion | flops 835191808 | bytes 28860416 | tf_op jit(solution)/shard_map/sub | solution.py:192
  224.8 33.6 %fusion.108 = (f32[12,512]{1,0:T(8,128)S(1)}, f32[12,512,1024]{2,1,0:T(8,128)}) fusion(f32[12,512,1024]{2,1,0:T(8,128)} %fusion.62, pred[512,1024]{1,0:T(8,128)(4,1)} %get-tuple-element.89), kind=kOutput, calls=%fused_computation.204 | output fusion | flops 37749760 | bytes 50880512 | tf_op jit(solution)/shard_map/sub | solution.py:192
  258.4 11.4 %fusion.52 = bf16[512,12,64]{0,2,1:T(8,128)(2,1)} fusion(bf16[1024,12,64]{0,2,1:T(8,128)(2,1)S(1)} %bitcast.72, f32[12,512,1024]{2,1,0:T(8,128)} %get-tuple-element.101, f32[12,512]{1,0:T(8,128)S(1)} %get-tuple-element.100), kind=kOutput, calls=%fused_computation.115 | convolution fusion | flops 818282496 | bytes 27549696 | tf_op jit(solution)/shard_map/hqk,khd->qhd/dot_general | solution.py:195
  269.7 11.6 %fusion.49 = bf16[512,12,64]{0,2,1:T(8,128)(2,1)} fusion(bf16[1024,12,64]{0,2,1:T(8,128)(2,1)S(1)} %bitcast.73, f32[12,512,1024]{2,1,0:T(8,128)} %get-tuple-element.99, f32[12,512]{1,0:T(8,128)S(1)} %get-tuple-element.98), kind=kOutput, calls=%fused_computation.114 | convolution fusion | flops 818282496 | bytes 27549696 | tf_op jit(solution)/shard_map/hqk,khd->qhd/dot_general | solution.py:195
  281.3 14.2 %all-gather.21.cloned.1.call-done = bf16[1,8192,768]{2,1,0:T(8,128)(2,1)} async-done(((bf16[1,1024,768]{2,1,0:T(8,128)(2,1)}), bf16[1,8192,768]{2,1,0:T(8,128)(2,1)}) %all-gather.21.cloned.1.call-update) | async-done | bytes 12582928 | tf_op jit(solution)/shard_map/all_gather | solution.py:212
  295.5 11.8 %gather_fusion.2 = bf16[1024,768]{1,0:T(8,128)(2,1)} fusion(bf16[8192,768]{1,0:T(8,128)(2,1)} %bitcast.68, s32[1024]{0:T(1024)S(1)} %get-tuple-element.93), kind=kCustom, calls=%fused_computation.2.clone | custom fusion | bytes 3149824 | tf_op jit(solution)/shard_map/jit(_take)/gather | solution.py:96
  312.2 10.9 %all-gather.15.cloned.1.call-done = bf16[768,768]{1,0:T(8,128)(2,1)} async-done(((bf16[192,768]{1,0:T(8,128)(2,1)}), bf16[768,768]{1,0:T(8,128)(2,1)}) %all-gather.15.cloned.1.call-update) | async-done | bytes 1179664 | tf_op jit(solution)/shard_map/all_gather | solution.py:149
  328.6 44.1 %all-gather.17.cloned.1.call-done = bf16[768,2304]{1,0:T(8,128)(2,1)} async-done(((bf16[192,2304]{1,0:T(8,128)(2,1)}), bf16[768,2304]{1,0:T(8,128)(2,1)}) %all-gather.17.cloned.1.call-update) | async-done | bytes 3538960 | tf_op jit(solution)/shard_map/all_gather | solution.py:151
  372.7 10.6 %fusion.93 = f32[1024,2304]{1,0:T(8,128)} fusion(bf16[768,2304]{1,0:T(8,128)(2,1)} %all-gather.17.cloned.1.call-done, f32[1024,768]{0,1:T(8,128)} %copy-done.12, f32[768]{0:T(1024)S(1)} %convert_element_type.186, f32[1024]{0:T(1024)S(1)} %fusion.73, f32[1024]{0:T(1024)S(1)} %broadcast_multiply_fusion), kind=kOutput, calls=%fused_computation.196 | convolution fusion | flops 3627024384 | bytes 16133120 | tf_op jit(solution)/shard_map/dot_general | solution.py:204
  383.3 23.8 %all-gather.19.cloned.1.call-done = bf16[1152,768]{1,0:T(8,128)(2,1)} async-done(((bf16[288,768]{1,0:T(8,128)(2,1)}), bf16[1152,768]{1,0:T(8,128)(2,1)}) %all-gather.19.cloned.1.call-update) | async-done | bytes 1769488 | tf_op jit(solution)/shard_map/all_gather | solution.py:152
  407.1 14.5 %fusion.42 = (f32[1024,1152]{1,0:T(8,128)}, f32[1024,1152]{1,0:T(8,128)S(1)}, f32[1024,1152]{1,0:T(8,128)S(1)}) fusion(f32[1024,2304]{1,0:T(8,128)} %fusion.93, bf16[1152,768]{1,0:T(8,128)(2,1)} %all-gather.19.cloned.1.call-done, bf16[1024,768]{0,1:T(8,128)(2,1)S(1)} %copy.75, pred[1024]{0:T(1024)(128)(4,1)S(1)} %get-tuple-element.85, ...), kind=kOutput, calls=%fused_computation.111 | convolution fusion | flops 1890189312 | bytes 22218752 | tf_op jit(solution)/shard_map/td,fd->tf/dot_general | solution.py:224
  451.5 19.3 %multiply_reduce_fusion.1 = (f32[12,512]{1,0:T(8,128)S(1)}, f32[12,512,1024]{2,1,0:T(8,128)}) fusion(f32[12,512,1024]{2,1,0:T(8,128)} %get-tuple-element.101, f32[12,512]{1,0:T(8,128)S(1)} %get-tuple-element.100, bf16[512,12,64]{0,2,1:T(8,128)(2,1)S(1)} %bitcast.82, bf16[1024,12,64]{0,2,1:T(8,128)(2,1)S(1)} %bitcast.74), kind=kOutput, calls=%fused_computation.9 | convolution fusion | flops 824174592 | bytes 52740096 | tf_op jit(solution)/shard_map/qhd,khd->hqk/dot_general | solution.py:257
  470.8 19.1 %multiply_reduce_fusion = (f32[12,512]{1,0:T(8,128)S(1)}, f32[12,512,1024]{2,1,0:T(8,128)}) fusion(f32[12,512,1024]{2,1,0:T(8,128)} %get-tuple-element.99, f32[12,512]{1,0:T(8,128)S(1)} %get-tuple-element.98, bf16[512,12,64]{0,2,1:T(8,128)(2,1)S(1)} %bitcast.84, bf16[1024,12,64]{0,2,1:T(8,128)(2,1)S(1)} %bitcast.75), kind=kOutput, calls=%fused_computation.7 | convolution fusion | flops 824174592 | bytes 52740096 | tf_op jit(solution)/shard_map/qhd,khd->hqk/dot_general | solution.py:257
  490.0 17.0 %multiply_convert_fusion.1 = bf16[12,512,1024]{2,1,0:T(8,128)(2,1)S(1)} fusion(f32[12,512,1024]{2,1,0:T(8,128)} %get-tuple-element.109, f32[12,512]{1,0:T(8,128)S(1)} %get-tuple-element.108, f32[12,512,1024]{2,1,0:T(8,128)} %get-tuple-element.101, f32[12,512]{1,0:T(8,128)S(1)} %get-tuple-element.100), kind=kLoop, calls=%fused_computation.8 | loop fusion | flops 25165824 | bytes 62963712 | tf_op jit(solution)/shard_map/convert_element_type | solution.py:261
  507.0 27.2 %multiply_convert_fusion = bf16[12,512,1024]{2,1,0:T(8,128)(2,1)} fusion(f32[12,512,1024]{2,1,0:T(8,128)} %get-tuple-element.107, f32[12,512]{1,0:T(8,128)S(1)} %get-tuple-element.106, f32[12,512,1024]{2,1,0:T(8,128)} %get-tuple-element.99, f32[12,512]{1,0:T(8,128)S(1)} %get-tuple-element.98), kind=kLoop, calls=%fused_computation.6 | loop fusion | flops 25165824 | bytes 62963712 | tf_op jit(solution)/shard_map/convert_element_type | solution.py:261
  578.3 10.6 %fusion.10 = f32[12,64,1024]{2,1,0:T(8,128)S(1)} fusion(bf16[512,12,64]{0,2,1:T(8,128)(2,1)S(1)} %bitcast.85, f32[12,512,1024]{2,1,0:T(8,128)} %get-tuple-element.99, f32[12,512]{1,0:T(8,128)S(1)} %get-tuple-element.98), kind=kOutput, calls=%fused_computation.26 | convolution fusion | flops 817889280 | bytes 29122560 | tf_op jit(solution)/shard_map/hqk,qhd->khd/dot_general | solution.py:273
  589.1 10.7 %add_convert_fusion.2 = bf16[12,64,1024]{2,1,0:T(8,128)(2,1)S(1)} fusion(f32[12,64,1024]{2,1,0:T(8,128)S(1)} %fusion.10, bf16[512,12,64]{0,2,1:T(8,128)(2,1)S(1)} %bitcast.83, f32[12,512,1024]{2,1,0:T(8,128)} %get-tuple-element.101, f32[12,512]{1,0:T(8,128)S(1)} %get-tuple-element.100), kind=kOutput, calls=%fused_computation.76 | convolution fusion | flops 819462144 | bytes 30695424 | tf_op jit(solution)/shard_map/hqk,qhd->khd/dot_general | solution.py:273
  609.8 10.6 %reduce-scatter.9.cloned.1.call-done = bf16[192,2304]{1,0:T(8,128)(2,1)} async-done(((bf16[768,2304]{1,0:T(8,128)(2,1)}), bf16[192,2304]{1,0:T(8,128)(2,1)}) %reduce-scatter.9.cloned.1.call-update) | async-done | bytes 884752 | tf_op jit(solution)/shard_map/reduce_scatter | solution.py:319
  620.3 50.2 %reduce-scatter.5.cloned.1.call-done = bf16[192,2304]{1,0:T(8,128)(2,1)} async-done(((bf16[768,2304]{1,0:T(8,128)(2,1)}), bf16[192,2304]{1,0:T(8,128)(2,1)}) %reduce-scatter.5.cloned.1.call-update) | async-done | bytes 884752 | tf_op jit(solution)/shard_map/reduce_scatter | solution.py:310
  699.6 14.8 %all-reduce.10 = (bf16[192]{0:T(256)(128)(2,1)S(1)}, bf16[192]{0:T(256)(128)(2,1)S(1)}) all-reduce(bf16[192]{0:T(256)(128)(2,1)S(1)} %dynamic-slice.4, bf16[192]{0:T(256)(128)(2,1)S(1)} %dynamic-slice.6), channel_id=1, replica_groups=mesh['replica'=8,'group'=4] {'replica'}, use_global_device_ids=true, to_apply=%region_24.26 | all-reduce | flops 384 | bytes 1536 | tf_op jit(solution)/shard_map/psum | solution.py:327
  715.5 26.3 %all-reduce.16.cloned.1.call-done = (bf16[192,2304]{1,0:T(8,128)(2,1)}, bf16[192,768]{1,0:T(8,128)(2,1)}, bf16[192,2304]{1,0:T(8,128)(2,1)}, bf16[288,768]{1,0:T(8,128)(2,1)}) async-done(((bf16[192,2304]{1,0:T(8,128)(2,1)}, bf16[192,768]{1,0:T(8,128)(2,1)}, bf16[192,2304]{1,0:T(8,128)(2,1)}, bf16[288,768]{1,0:T(8,128)(2,1)}), (bf16[192,2304]{1,0:T(8,128)(2,1)}, bf16[192,768]{1,0:T(8,128)(2,1)}, ...) | async-done | bytes 2506768 | tf_op jit(solution)/shard_map/psum | solution.py:328
  748.5 111.2 %all-gather.23.cloned.1.call-done = bf16[8192,768]{0,1:T(8,128)(2,1)} async-done(((bf16[1024,768]{0,1:T(8,128)(2,1)}), bf16[8192,768]{0,1:T(8,128)(2,1)}) %all-gather.23.cloned.1.call-update) | async-done | bytes 12582928 | tf_op jit(solution)/shard_map/all_gather | solution.py:210
  859.7 16.7 %copy.73 = bf16[8192,768]{1,0:T(8,128)(2,1)} copy(bf16[8192,768]{0,1:T(8,128)(2,1)} %all-gather.23.cloned.1.call-done) | data formatting | bytes 25165824 | tf_op jit(solution)/shard_map/all_gather | solution.py:210
  876.3 10.8 %gather_fusion.1 = bf16[1024,768]{1,0:T(8,128)(2,1)S(1)} fusion(bf16[8192,768]{1,0:T(8,128)(2,1)} %copy.73, s32[1024]{0:T(1024)S(1)} %fusion.75), kind=kCustom, calls=%fused_computation.1.clone | custom fusion | bytes 3149824 | tf_op jit(solution)/shard_map/jit(_take)/gather | solution.py:96
  887.9 89.0 %all-gather.25.cloned.1.call-done = bf16[8192,768]{0,1:T(8,128)(2,1)} async-done(((bf16[1024,768]{0,1:T(8,128)(2,1)}), bf16[8192,768]{0,1:T(8,128)(2,1)}) %all-gather.25.cloned.1.call-update) | async-done | bytes 12582928 | tf_op jit(solution)/shard_map/all_gather | solution.py:296
  976.9 16.7 %copy.76 = bf16[8192,768]{1,0:T(8,128)(2,1)} copy(bf16[8192,768]{0,1:T(8,128)(2,1)} %all-gather.25.cloned.1.call-done) | data formatting | bytes 25165824 | tf_op jit(solution)/shard_map/all_gather | solution.py:296
  993.5 11.8 %gather_fusion.3 = bf16[1024,768]{1,0:T(8,128)(2,1)} fusion(bf16[8192,768]{1,0:T(8,128)(2,1)} %copy.76, s32[1024]{0:T(1024)S(1)} %fusion.75), kind=kCustom, calls=%fused_computation.3.clone | custom fusion | bytes 3149824 | tf_op jit(solution)/shard_map/jit(_take)/gather | solution.py:96
  (261 shorter events, 179.2 us)
Async XLA Ops:
  7.2 122.0 %all-gather.11.cloned.1.call-start = ((), (), s32[]{:S(2)}) async-start(), calls=%async_computation.4 | async-start | bytes 14155776 | tf_op jit(solution)/shard_map/all_gather | solution.py:155
  7.9 169.1 %all-gather.13.cloned.1.call-start = ((), (), s32[]{:S(2)}) async-start(), calls=%async_computation.5 | async-start | bytes 4423680 | tf_op jit(solution)/shard_map/all_gather | solution.py:148
  10.6 284.9 %all-gather.21.cloned.1.call-start = ((), (), s32[]{:S(2)}) async-start(), calls=%async_computation.9 | async-start | bytes 14155776 | tf_op jit(solution)/shard_map/all_gather | solution.py:212
  11.4 311.8 %all-gather.15.cloned.1.call-start = ((), (), s32[]{:S(2)}) async-start(), calls=%async_computation.6 | async-start | bytes 1474560 | tf_op jit(solution)/shard_map/all_gather | solution.py:149
  12.2 360.5 %all-gather.17.cloned.1.call-start = ((), (), s32[]{:S(2)}) async-start(), calls=%async_computation.7 | async-start | bytes 4423680 | tf_op jit(solution)/shard_map/all_gather | solution.py:151
  13.3 393.7 %all-gather.19.cloned.1.call-start = ((), (), s32[]{:S(2)}) async-start(), calls=%async_computation.8 | async-start | bytes 2211840 | tf_op jit(solution)/shard_map/all_gather | solution.py:152
  14.2 595.5 %reduce-scatter.7.cloned.1.call-start = ((), (), s32[]{:S(2)}) async-start(), calls=%async_computation.11 | async-start | bytes 1474560 | tf_op jit(solution)/shard_map/reduce_scatter | solution.py:313
  19.6 421.3 %copy-start.53 = (pred[1024]{0:T(1024)(128)(4,1)}, pred[1024]{0:T(1024)(128)(4,1)S(1)}, u32[]{:S(2)}) copy-start(pred[1024]{0:T(1024)(128)(4,1)S(1)} %get-tuple-element.84) | copy-start | bytes 3076
  19.7 421.3 %copy-start.55 = (pred[1024]{0:T(1024)(128)(4,1)}, pred[1024]{0:T(1024)(128)(4,1)S(1)}, u32[]{:S(2)}) copy-start(pred[1024]{0:T(1024)(128)(4,1)S(1)} %get-tuple-element.85) | copy-start | bytes 3076
  32.8 144.3 %copy-start.43 = (f32[768]{0:T(1024)}, f32[768]{0:T(1024)S(1)}, u32[]{:S(2)}) copy-start(f32[768]{0:T(1024)S(1)} %convert_element_type.173) | copy-start | bytes 9220
  33.4 162.4 %copy-start.29 = (f32[1024,32]{0,1:T(8,128)}, f32[1024,32]{0,1:T(8,128)S(1)}, u32[]{:S(2)}) copy-start(f32[1024,32]{0,1:T(8,128)S(1)} %get-tuple-element.86) | copy-start | bytes 393220
  33.4 162.4 %copy-start.31 = (f32[1024,32]{0,1:T(8,128)}, f32[1024,32]{0,1:T(8,128)S(1)}, u32[]{:S(2)}) copy-start(f32[1024,32]{0,1:T(8,128)S(1)} %get-tuple-element.87) | copy-start | bytes 393220
  140.6 182.6 %copy-start.1 = (bf16[1024,768]{0,1:T(8,128)(2,1)}, bf16[1024,768]{0,1:T(8,128)(2,1)S(1)}, u32[]{:S(2)}) copy-start(bf16[1024,768]{0,1:T(8,128)(2,1)S(1)} %copy.68) | copy-start | bytes 4718596
  141.1 36.0 %copy-start.41 = (f32[1024]{0:T(1024)}, f32[1024]{0:T(1024)S(1)}, u32[]{:S(2)}) copy-start(f32[1024]{0:T(1024)S(1)} %broadcast_multiply_fusion.1) | copy-start | bytes 12292
  141.7 35.4 %copy-start.49 = (f32[1024]{0:T(1024)}, f32[1024]{0:T(1024)S(1)}, u32[]{:S(2)}) copy-start(f32[1024]{0:T(1024)S(1)} %fusion.33) | copy-start | bytes 12292
  141.7 35.3 %copy-start.45 = (f32[1024]{0:T(1024)}, f32[1024]{0:T(1024)S(1)}, u32[]{:S(2)}) copy-start(f32[1024]{0:T(1024)S(1)} %fusion.72) | copy-start | bytes 12292
  224.8 33.6 %copy-start.24 = (bf16[1024,768]{0,1:T(8,128)(2,1)S(1)}, bf16[1024,768]{0,1:T(8,128)(2,1)}, u32[]{:S(2)}) copy-start(bf16[1024,768]{0,1:T(8,128)(2,1)} %copy.69) | copy-start | bytes 4718596
  309.0 98.1 %copy-start.5 = (bf16[1024,768]{0,1:T(8,128)(2,1)}, bf16[1024,768]{0,1:T(8,128)(2,1)S(1)}, u32[]{:S(2)}) copy-start(bf16[1024,768]{0,1:T(8,128)(2,1)S(1)} %copy.75) | copy-start | bytes 4718596
  407.1 14.5 %copy-start.19 = (f32[1024,2304]{1,0:T(8,128)S(1)}, f32[1024,2304]{1,0:T(8,128)}, u32[]{:S(2)}) copy-start(f32[1024,2304]{1,0:T(8,128)} %fusion.93) | copy-start | bytes 28311556
  449.6 21.1 %copy-start.35 = (bf16[512,768]{0,1:T(8,128)(2,1)}, bf16[512,768]{0,1:T(8,128)(2,1)S(1)}, u32[]{:S(2)}) copy-start(bf16[512,768]{0,1:T(8,128)(2,1)S(1)} %get-tuple-element.78) | copy-start | bytes 2359300
  449.7 21.1 %copy-start.37 = (bf16[512,768]{0,1:T(8,128)(2,1)}, bf16[512,768]{0,1:T(8,128)(2,1)S(1)}, u32[]{:S(2)}) copy-start(bf16[512,768]{0,1:T(8,128)(2,1)S(1)} %get-tuple-element.79) | copy-start | bytes 2359300
  449.7 160.1 %reduce-scatter.11.cloned.1.call-start = ((), (), s32[]{:S(2)}) async-start(), calls=%async_computation.13 | async-start | bytes 2211840 | tf_op jit(solution)/shard_map/reduce_scatter | solution.py:322
  489.9 130.4 %reduce-scatter.9.cloned.1.call-start = ((), (), s32[]{:S(2)}) async-start(), calls=%async_computation.12 | async-start | bytes 4423680 | tf_op jit(solution)/shard_map/reduce_scatter | solution.py:319
  507.0 27.2 %copy-start = (bf16[12,512,1024]{2,1,0:T(8,128)(2,1)}, bf16[12,512,1024]{2,1,0:T(8,128)(2,1)S(1)}, u32[]{:S(2)}) copy-start(bf16[12,512,1024]{2,1,0:T(8,128)(2,1)S(1)} %multiply_convert_fusion.1) | copy-start | bytes 37748740
  507.0 27.2 %copy-start.9 = (bf16[1024,12,32]{0,2,1:T(8,128)(2,1)S(1)}, bf16[1024,12,32]{0,2,1:T(8,128)(2,1)}, u32[]{:S(2)}) copy-start(bf16[1024,12,32]{0,2,1:T(8,128)(2,1)} %copy-done.8) | copy-start | bytes 2359300
  507.0 27.2 %copy-start.11 = (bf16[1024,12,32]{0,2,1:T(8,128)(2,1)S(1)}, bf16[1024,12,32]{0,2,1:T(8,128)(2,1)}, u32[]{:S(2)}) copy-start(bf16[1024,12,32]{0,2,1:T(8,128)(2,1)} %copy-done.10) | copy-start | bytes 2359300
  572.9 97.6 %reduce-scatter.5.cloned.1.call-start = ((), (), s32[]{:S(2)}) async-start(), calls=%async_computation.10 | async-start | bytes 4423680 | tf_op jit(solution)/shard_map/reduce_scatter | solution.py:310
  578.3 21.4 %copy-start.27 = (bf16[1024,12,64]{0,2,1:T(8,128)(2,1)}, bf16[1024,12,64]{0,2,1:T(8,128)(2,1)S(1)}, u32[]{:S(2)}) copy-start(bf16[1024,12,64]{0,2,1:T(8,128)(2,1)S(1)} %add_convert_fusion.3) | copy-start | bytes 4718596
  589.0 11.9 %copy-start.2 = (bf16[1024,768]{0,1:T(8,128)(2,1)S(1)}, bf16[1024,768]{0,1:T(8,128)(2,1)}, u32[]{:S(2)}) copy-start(bf16[1024,768]{0,1:T(8,128)(2,1)} %copy-done.1) | copy-start | bytes 4718596
  609.7 132.1 %all-reduce.16.cloned.1.call-start = ((), (), s32[]{:S(2)}) async-start(), calls=%async_computation.16 | async-start | bytes 5013504 | tf_op jit(solution)/shard_map/psum | solution.py:328
  670.5 189.1 %all-gather.23.cloned.1.call-start = ((), (), s32[]{:S(2)}) async-start(), calls=%async_computation.14 | async-start | bytes 14155776 | tf_op jit(solution)/shard_map/all_gather | solution.py:210
  677.2 299.7 %all-gather.25.cloned.1.call-start = ((), (), s32[]{:S(2)}) async-start(), calls=%async_computation.15 | async-start | bytes 14155776 | tf_op jit(solution)/shard_map/all_gather | solution.py:296
  (49 other events, 259.5 us)
Sparse Core Ops, SparseCore 0:
  9.7 119.4 all-gather.10
  131.6 45.4 all-gather.12
  178.7 116.7 all-gather.20
  297.2 25.9 all-gather.14
  325.4 47.2 all-gather.16
  374.4 32.5 all-gather.18
  449.8 28.5 reduce-scatter.6
  490.0 32.4 reduce-scatter.10
  573.1 47.2 reduce-scatter.8
  623.2 47.2 reduce-scatter.4
  673.2 68.5 all-reduce.15
  743.3 116.2 all-gather.22
  861.9 114.9 all-gather.24
where the time goes:
time: 1030 us; the launch traced here: 1020 us
  waiting for transfers between devices  511 us (50%)
  matrix products  222 us (22%)
  other arithmetic  122 us (12%)
  local copies, waits for them, and re-layouts  113 us (11%)
  blocking collectives  35 us (3%)
  between operations  16.4 us (2%)
    all_gather x1, waiting for transfers between devices, on_device(): lax.all_gather(output_dealt[None], 'replica', axis=1, tiled=True)  111 us
    all_gather x1, waiting for transfers between devices, on_device(): lax.all_gather(tokens, 'replica', axis=1, tiled=True)  94.1 us
    all_gather x1, waiting for transfers between devices, on_device(): lax.all_gather(grad_input[None], 'replica', axis=1, tiled=True)  89 us
    reduce_scatter x1, waiting for transfers between devices, on_device(): lax.psum_scatter(partial_grads[1].astype(jnp.bfloat16), 'group', scatter_...  50.2 us
    gather x8, local copies, waits for them, and re-layouts, pick_rows(): taken = jnp.take(piece[0], jnp.clip(index_map, 0, piece_rows - 1), axis=0)  49.9 us
    convert_element_type x2, other arithmetic, on_device(): grad_scores = (weights_full * (grad_probs - inner)).astype(jnp.bfloat16)  44.2 us
    all_gather x1, waiting for transfers between devices, on_device(): lax.all_gather(masters[4], 'group', axis=0, tiled=True)  44.1 us
    dot_general x2, matrix products, on_device(): jnp.einsum('qhd,khd->hqk', grad_block, value_heads, preferred_element_typ...  38.4 us
  transfers between devices with their start and end apart: 13, of which 11 were waited for; matrix products, arithmetic and copies ran while one was open for 36% of the time, Pallas kernels for 0%

commit v1 on v0

v1 whole, which is shorter than its diff:
```python
import functools
import math

import jax
import jax.numpy as jnp
from jax import lax
from jax.experimental import pallas as pl
from jax.experimental.pallas import tpu as pltpu
from jax.sharding import PartitionSpec as P

HEADS = 12
HEAD_DIM = 64
LANES = 128
HALO = 768
RB = 256
QB = 128
KB = 256
EPS = 1e-05
BIG = -1e30
ROPE_BASE = 160000.0
LOG2E = 1.4426950408889634
LN2 = 0.6931471805599453
BF = jnp.bfloat16
F32 = jnp.float32
VMEM = 60 * 1024 * 1024


def nt(a, b):
    return lax.dot_general(a, b, (((1,), (1,)), ((), ())), preferred_element_type=F32)


def nn(a, b):
    return lax.dot_general(a, b, (((1,), (0,)), ((), ())), preferred_element_type=F32)


def partner(x):
    lane = lax.broadcasted_iota(jnp.int32, x.shape, 1) % HEAD_DIM
    return jnp.where(lane < HEAD_DIM // 2, pltpu.roll(x, 96, 1), pltpu.roll(x, 32, 1))


def params(**kw):
    return pltpu.CompilerParams(vmem_limit_bytes=VMEM, **kw)


def plan(lengths, replica, n_replica, tok):
    ext = tok + 2 * HALO + RB
    n_seq = lengths.shape[0]
    order = jnp.arange(n_seq, dtype=jnp.int32)
    starts = jnp.sum(jnp.where(order[None, :] < order[:, None], lengths[None, :], 0), axis=1)
    ends = starts + lengths
    total = n_replica * tok
    base = replica * tok - HALO

    def look(g):
        seg = jnp.sum((g[:, None] >= starts[None, :]).astype(jnp.int32), axis=1) - 1
        seg = seg + (g >= total).astype(jnp.int32)
        first = jnp.max(jnp.where(g[:, None] >= starts[None, :], starts[None, :], 0), axis=1)
        last = jnp.min(jnp.where(g[:, None] < ends[None, :], ends[None, :], total), axis=1)
        return seg, first, last

    rows = base + jnp.arange(ext, dtype=jnp.int32)
    seg, first, _ = look(rows)
    pos = jnp.maximum(rows - first, 0)
    n_qb = (tok + 2 * HALO) // QB
    heads_of = base + jnp.arange(n_qb, dtype=jnp.int32) * QB
    _, f0, l0 = look(heads_of)
    _, f1, l1 = look(heads_of + (QB - 1))
    own_lo, own_hi = HALO, HALO + tok
    _, fe, le = look(base + jnp.array([own_lo, own_hi - 1], dtype=jnp.int32))
    lo_e, hi_e = fe[0] - base, le[1] - base
    idx = jnp.arange(n_qb, dtype=jnp.int32)
    left, right = idx < own_lo // QB, idx >= own_hi // QB
    k_lo = jnp.where(left, own_lo, jnp.where(right, fe[1] - base, f0 - base))
    k_hi = jnp.where(left, le[0] - base, jnp.where(right, own_hi, l1 - base))
    k_lo = k_lo // QB
    k_n = (k_hi - k_lo * QB + (KB - 1)) // KB
    q_lo, q_hi = lo_e // QB, (hi_e + QB - 1) // QB
    blk = jnp.arange(ext // RB, dtype=jnp.int32) * RB
    need = ((blk + RB > lo_e) & (blk < hi_e)).astype(jnp.int32)
    scal = jnp.concatenate([k_lo, k_n, jnp.stack([q_lo, q_hi]), need])
    return seg, pos, scal


def features(seg):
    lane = jnp.arange(LANES, dtype=jnp.int32)
    hot = (seg[:, None] & 15) == lane[None, :]
    qf = jnp.where(hot, BIG, 0.0).astype(BF)
    kf = jnp.where(hot | (lane >= 16)[None, :], 0.0, 1.0).astype(BF)
    return qf, kf


def rope_tables(pos):
    half = HEAD_DIM // 2
    lane = jnp.arange(LANES, dtype=jnp.int32)
    freq = jnp.exp(-((lane % half).astype(F32) * (2.0 / HEAD_DIM)) * math.log(ROPE_BASE))
    ang = pos.astype(F32)[:, None] * freq[None, :]
    sign = jnp.where(lane % HEAD_DIM < half, -1.0, 1.0).astype(F32)
    return jnp.cos(ang), jnp.sin(ang) * sign[None, :]


def qkv_kernel(n_qb, own_b, need_off, scal, xl, xc, xr, w, g1, cos, sin, qkv, kt, vt, n1o):
    i = pl.program_id(0)
    left_b = HALO // RB

    @pl.when(scal[need_off + i] == 0)
    def _():
        qkv[...] = jnp.zeros_like(qkv)
        kt[...] = jnp.zeros_like(kt)
        vt[...] = jnp.zeros_like(vt)

    @pl.when(scal[need_off + i] != 0)
    def _():
        x = jnp.where(i < left_b, xl[...], jnp.where(i < left_b + own_b, xc[...], xr[...])).astype(F32)
        mean = jnp.mean(x, axis=-1, keepdims=True)
        cen = x - mean
        var = jnp.mean(cen * cen, axis=-1, keepdims=True)
        n1 = (cen * lax.rsqrt(var + EPS) * g1[...]).astype(BF)

        @pl.when((i >= left_b) & (i < left_b + own_b))
        def _():
            n1o[...] = n1

        width = n1.shape[1]
        co, si = cos[...], sin[...]
        sc = HEAD_DIM ** -0.5 * LOG2E
        cq, sq = co * sc, si * sc
        for c in range(3 * width // 256):
            a = nn(n1, w[:, 256 * c : 256 * c + 256])
            part = 256 * c // width
            if part < 2:
                cc, ss = (cq, sq) if part == 0 else (co, si)
                halves = []
                for h in range(2):
                    b = a[:, 128 * h : 128 * h + 128]
                    halves.append((b * cc + partner(b) * ss).astype(BF))
                r = jnp.concatenate(halves, axis=1)
            else:
                r = a.astype(BF)
            qkv[:, 256 * c : 256 * c + 256] = r
            off = 256 * c - width * part
            if part == 1:
                kt[off : off + 256, :] = r.T
            if part == 2:
                vt[off : off + 256, :] = r.T


def qkv_call(scal, xl, xc, xr, w, g1, cos, sin, n_qb):
    tok, width = xc.shape
    ext = cos.shape[0]
    own_b, lb = tok // RB, HALO // RB
    blocks = ext // RB
    need_off = 2 * n_qb + 2
    clampi = lambda lo, n: (lambda i, s: (jnp.clip(i - lo, 0, n - 1), 0))
    row = lambda i, s: (i, 0)
    fix = lambda i, s: (0, 0)
    col = lambda i, s: (0, i)
    return pl.pallas_call(
        functools.partial(qkv_kernel, n_qb, own_b, need_off),
        grid_spec=pltpu.PrefetchScalarGridSpec(
            num_scalar_prefetch=1,
            grid=(blocks,),
            in_specs=[
                pl.BlockSpec((RB, width), clampi(0, lb)),
                pl.BlockSpec((RB, width), clampi(lb, own_b)),
                pl.BlockSpec((RB, width), clampi(lb + own_b, lb)),
                pl.BlockSpec((width, 3 * width), fix),
                pl.BlockSpec((1, width), fix),
                pl.BlockSpec((RB, LANES), row),
                pl.BlockSpec((RB, LANES), row),
            ],
            out_specs=[
                pl.BlockSpec((RB, 3 * width), row),
                pl.BlockSpec((width, RB), col),
                pl.BlockSpec((width, RB), col),
                pl.BlockSpec((RB, width), clampi(lb, own_b)),
            ],
        ),
        out_shape=[
            jax.ShapeDtypeStruct((ext, 3 * width), BF),
            jax.ShapeDtypeStruct((width, ext), BF),
            jax.ShapeDtypeStruct((width, ext), BF),
            jax.ShapeDtypeStruct((tok, width), BF),
        ],
        compiler_params=params(dimension_semantics=("arbitrary",)),
        cost_estimate=pl.CostEstimate(flops=2 * 2000 * width * 3 * width, bytes_accessed=30_000_000, transcendentals=0),
        name="qkv",
    )(scal, xl, xc, xr, w, g1, cos, sin)


def split_heads(x):
    low = lax.broadcasted_iota(jnp.int32, x.shape, 1) < HEAD_DIM
    zero = jnp.zeros_like(x)
    return jnp.concatenate([jnp.where(low, x, zero), jnp.where(low, zero, x)], axis=0)


def fwd_kernel(pg, n_qb, tok, scal, q, k, vt, qf, kf, out, lse, q2, s_buf):
    first_qb = HALO // QB
    ones = jnp.ones((16, KB), BF)

    def per_q(qi, _):
        qb = first_qb + qi
        r0 = pl.multiple_of(qb * QB, QB)
        o0 = pl.multiple_of(qi * QB, QB)
        k_lo, k_n = scal[qb], scal[n_qb + qb]
        fq = qf[pl.ds(r0, QB), :]
        f2 = jnp.concatenate([fq, fq], axis=0)
        for p in range(pg):
            both = split_heads(q[pl.ds(r0, QB), LANES * p : LANES * p + LANES])
            q2[p] = jnp.concatenate([both, f2], axis=1)

        def scores(t, tops):
            k0 = pl.multiple_of(k_lo * QB + t * KB, QB)
            fk = kf[pl.ds(k0, KB), :]
            new = []
            for p in range(pg):
                kk = jnp.concatenate([k[pl.ds(k0, KB), LANES * p : LANES * p + LANES], fk], axis=1)
                s = nt(kk, q2[p])
                s_buf[p, pl.ds(pl.multiple_of(t * KB, KB), KB), :] = s
                new.append(jnp.maximum(tops[p], jnp.max(s.reshape(KB // 8, 8, 2 * QB), axis=0)))
            return tuple(new)

        tops = lax.fori_loop(0, k_n, scores, tuple(jnp.full((8, 2 * QB), BIG, F32) for _ in range(pg)))
        tops = [jnp.max(t, axis=0, keepdims=True) for t in tops]

        def mix(t, accs):
            k0 = pl.multiple_of(k_lo * QB + t * KB, QB)
            new = []
            for p in range(pg):
                s = s_buf[p, pl.ds(pl.multiple_of(t * KB, KB), KB), :]
                pb = jnp.exp2(s - tops[p]).astype(BF)
                va = jnp.concatenate([vt[LANES * p : LANES * p + LANES, pl.ds(k0, KB)], ones], axis=0)
                new.append(accs[p] + nn(va, pb))
            return tuple(new)

        accs = lax.fori_loop(0, k_n, mix, tuple(jnp.zeros((LANES + 16, 2 * QB), F32) for _ in range(pg)))
        for p in range(pg):
            acc = accs[p]
            total = acc[LANES : LANES + 1, :]
            inv = 1.0 / total
            o_t = jnp.concatenate([acc[:HEAD_DIM, :QB] * inv[:, :QB], acc[HEAD_DIM:LANES, QB:] * inv[:, QB:]], axis=0)
            out[pl.ds(o0, QB), LANES * p : LANES * p + LANES] = o_t.T.astype(BF)
            st = tops[p] + jnp.log2(total)
            lse[p, 0:1, pl.ds(o0, QB)] = st[:, :QB]
            lse[p, 1:2, pl.ds(o0, QB)] = st[:, QB:]
        return 0

    lax.fori_loop(0, tok // QB, per_q, 0)


def fwd_call(scal, qkv, vt, qf, kf, tok, width, n_qb, pg):
    ext = qkv.shape[0]
    pairs = width // LANES
    steps = pairs // pg
    col = lambda off: (lambda i, s: (0, off + i))
    fix = lambda i, s: (0, 0)
    s_rows = -(-(QB + 2 * HALO) // KB) * KB + KB
    return pl.pallas_call(
        functools.partial(fwd_kernel, pg, n_qb, tok),
        grid_spec=pltpu.PrefetchScalarGridSpec(
            num_scalar_prefetch=1,
            grid=(steps,),
            in_specs=[
                pl.BlockSpec((ext, LANES * pg), col(0)),
                pl.BlockSpec((ext, LANES * pg), col(steps)),
                pl.BlockSpec((LANES * pg, ext), lambda i, s: (i, 0)),
                pl.BlockSpec((ext, LANES), fix),
                pl.BlockSpec((ext, LANES), fix),
            ],
            out_specs=[
                pl.BlockSpec((tok, LANES * pg), col(0)),
                pl.BlockSpec((pg, 2, tok), lambda i, s: (i, 0, 0)),
            ],
            scratch_shapes=[
                pltpu.VMEM((pg, 2 * QB, 2 * LANES), BF),
                pltpu.VMEM((pg, s_rows, 2 * QB), F32),
            ],
        ),
        out_shape=[
            jax.ShapeDtypeStruct((tok, width), BF),
            jax.ShapeDtypeStruct((pairs, 2, tok), F32),
        ],
        compiler_params=params(dimension_semantics=("arbitrary",)),
        cost_estimate=pl.CostEstimate(flops=30_000_000_000, bytes_accessed=15_000_000, transcendentals=0),
        name="attn_forward",
    )(scal, qkv, qkv, vt, qf, kf)


def mid_kernel(x, o, gy, wo, wi, wd, g2, ind, out, m_o, gu_o, n2_o, gh2_o, gh2b_o, go_o, dlt, dg2):
    ff = wd.shape[0]
    h2 = x[...].astype(F32) + nn(o[...], wo[...])
    mean = jnp.mean(h2, axis=-1, keepdims=True)
    cen = h2 - mean
    r2 = lax.rsqrt(jnp.mean(cen * cen, axis=-1, keepdims=True) + EPS)
    nh = cen * r2
    g = g2[...]
    n2 = (nh * g).astype(BF)
    n2_o[...] = n2
    gyb = gy[...]
    y = h2
    gn2 = jnp.zeros_like(h2)
    step = 384
    for c in range(ff // step):
        lo = c * step
        a = nn(n2, wi[:, lo : lo + step])
        b = nn(n2, wi[:, ff + lo : ff + lo + step])
        gm = nt(gyb, wd[lo : lo + step, :])
        half = 0.5 * (1.0 + lax.erf(a * (2.0 ** -0.5)))
        gel = a * half
        mm = (gel * b).astype(BF)
        m_o[:, lo : lo + step] = mm
        y = y + nn(mm, wd[lo : lo + step, :])
        dgel = half + a * (jnp.exp(-0.5 * a * a) * (1.0 / math.sqrt(2.0 * math.pi)))
        ga = (gm * b * dgel).astype(BF)
        gb = (gm * gel).astype(BF)
        gu_o[:, lo : lo + step] = ga
        gu_o[:, ff + lo : ff + lo + step] = gb
        gn2 = gn2 + nt(ga, wi[:, lo : lo + step]) + nt(gb, wi[:, ff + lo : ff + lo + step])
    out[...] = y.astype(BF)

    @pl.when(pl.program_id(0) == 0)
    def _():
        dg2[...] = jnp.zeros_like(dg2)

    dg2[...] += jnp.sum(gn2 * nh, axis=0, keepdims=True)
    t = gn2 * g
    gh2 = gyb.astype(F32) + r2 * (t - jnp.mean(t, axis=-1, keepdims=True) - nh * jnp.mean(t * nh, axis=-1, keepdims=True))
    gh2_o[...] = gh2
    gb16 = gh2.astype(BF)
    gh2b_o[...] = gb16
    go = nt(gb16, wo[...]).astype(BF)
    go_o[...] = go
    prod = go.astype(F32) * o[...].astype(F32)
    hi = prod.astype(BF)
    lo_part = (prod - hi.astype(F32)).astype(BF)
    dlt[...] = nt(ind[...], hi) + nt(ind[...], lo_part)


def mid_call(x, o, gy, wo, wi, wd, g2):
    tok, width = x.shape
    ff = wd.shape[0]
    heads = jnp.arange(16, dtype=jnp.int32)
    ind = (heads[:, None] == (jnp.arange(width, dtype=jnp.int32) // HEAD_DIM)[None, :]).astype(BF)
    row = lambda i: (i, 0)
    fix = lambda i: (0, 0)
    rs = lambda n: pl.BlockSpec((RB, n), row)
    fs = lambda a: pl.BlockSpec(a.shape, fix)
    sh = jax.ShapeDtypeStruct
    return pl.pallas_call(
        mid_kernel,
        grid=(tok // RB,),
        in_specs=[rs(width), rs(width), rs(width), fs(wo), fs(wi), fs(wd), fs(g2), fs(ind)],
        out_specs=[rs(width), rs(ff), rs(2 * ff), rs(width), rs(width), rs(width), rs(width),
                   pl.BlockSpec((16, RB), lambda i: (0, i)), pl.BlockSpec((1, width), fix)],
        out_shape=[sh((tok, width), BF), sh((tok, ff), BF), sh((tok, 2 * ff), BF), sh((tok, width), BF),
                   sh((tok, width), F32), sh((tok, width), BF), sh((tok, width), BF),
                   sh((16, tok), F32), sh((1, width), F32)],
        compiler_params=params(dimension_semantics=("arbitrary",)),
        cost_estimate=pl.CostEstimate(flops=13_000_000_000 * 2, bytes_accessed=30_000_000, transcendentals=0),
        name="middle",
    )(x, o, gy, wo, wi, wd, g2, ind)


def bwd_kernel(pg, n_qb, tok, scal, q, k, v, kt, qf, kf, gl, gc, gr, lse, dlt, cos, sin,
               gq_o, gk_o, gv_o, q2, g2, go, gka, gva):
    first_qb, last_qb = HALO // QB, (HALO + tok) // QB
    ext = q.shape[0]
    go[0:HALO, :] = gl[...]
    go[HALO : HALO + tok, :] = gc[...]
    go[HALO + tok : HALO + tok + HALO, :] = gr[...]
    gka[...] = jnp.zeros_like(gka)
    gva[...] = jnp.zeros_like(gva)
    sc = HEAD_DIM ** -0.5

    def per_q(qb, _):
        r0 = pl.multiple_of(qb * QB, QB)
        k_lo, k_n = scal[qb], scal[n_qb + qb]
        fq = qf[pl.ds(r0, QB), :]
        f2 = jnp.concatenate([fq, fq], axis=0)
        tops, dels = [], []
        for p in range(pg):
            both = split_heads(q[pl.ds(r0, QB), LANES * p : LANES * p + LANES])
            q2[p] = jnp.concatenate([both, f2], axis=1)
            g2[p] = split_heads(go[pl.ds(r0, QB), LANES * p : LANES * p + LANES])
            tops.append(jnp.concatenate([lse[p, 0:1, pl.ds(r0, QB)], lse[p, 1:2, pl.ds(r0, QB)]], axis=1))
            dels.append(jnp.concatenate([dlt[p, 0:1, pl.ds(r0, QB)], dlt[p, 1:2, pl.ds(r0, QB)]], axis=1))

        def body(t, accs):
            k0 = pl.multiple_of(k_lo * QB + t * KB, QB)
            fk = kf[pl.ds(k0, KB), :]
            new = []
            for p in range(pg):
                cols = slice(LANES * p, LANES * p + LANES)
                kk = jnp.concatenate([k[pl.ds(k0, KB), cols], fk], axis=1)
                pr = jnp.exp2(nt(kk, q2[p]) - tops[p])
                gp = nt(v[pl.ds(k0, KB), cols], g2[p])
                ds = (pr * (gp - dels[p])).astype(BF)
                gva[p, pl.ds(k0, KB), :] += nn(pr.astype(BF), g2[p])
                gka[p, pl.ds(k0, KB), :] += nn(ds, q2[p, :, :LANES])
                new.append(accs[p] + nn(kt[LANES * p : LANES * p + LANES, pl.ds(k0, KB)], ds))
            return tuple(new)

        accs = lax.fori_loop(0, k_n, body, tuple(jnp.zeros((LANES, 2 * QB), F32) for _ in range(pg)))

        @pl.when((qb >= first_qb) & (qb < last_qb))
        def _():
            o0 = pl.multiple_of((qb - first_qb) * QB, QB)
            co, si = cos[pl.ds(o0, QB), :] * sc, sin[pl.ds(o0, QB), :] * sc
            for p in range(pg):
                gt = jnp.concatenate([accs[p][:HEAD_DIM, :QB], accs[p][HEAD_DIM:, QB:]], axis=0).T
                gq_o[pl.ds(o0, QB), LANES * p : LANES * p + LANES] = (gt * co - partner(gt) * si).astype(BF)
        return 0

    lax.fori_loop(scal[2 * n_qb], scal[2 * n_qb + 1], per_q, 0)

    def finish(i, _):
        o0 = pl.multiple_of(i * QB, QB)
        r0 = pl.multiple_of(HALO + i * QB, QB)
        co, si = cos[pl.ds(o0, QB), :] * LN2, sin[pl.ds(o0, QB), :] * LN2
        for p in range(pg):
            cols = slice(LANES * p, LANES * p + LANES)
            a = gka[p, pl.ds(r0, QB), :]
            gk_o[pl.ds(o0, QB), cols] = (a * co - partner(a) * si).astype(BF)
            gv_o[pl.ds(o0, QB), cols] = gva[p, pl.ds(r0, QB), :].astype(BF)
        return 0

    lax.fori_loop(0, tok // QB, finish, 0)


def bwd_call(scal, qkv, kt, qf, kf, gl, gc, gr, lse, dlt, cos, sin, tok, width, n_qb, pg):
    ext = qkv.shape[0]
    pairs = width // LANES
    steps = pairs // pg
    col = lambda off: (lambda i, s: (0, off + i))
    fix = lambda i, s: (0, 0)
    wide = LANES * pg
    sh = jax.ShapeDtypeStruct
    return pl.pallas_call(
        functools.partial(bwd_kernel, pg, n_qb, tok),
        grid_spec=pltpu.PrefetchScalarGridSpec(
            num_scalar_prefetch=1,
            grid=(steps,),
            in_specs=[
                pl.BlockSpec((ext, wide), col(0)),
                pl.BlockSpec((ext, wide), col(steps)),
                pl.BlockSpec((ext, wide), col(2 * steps)),
                pl.BlockSpec((wide, ext), lambda i, s: (i, 0)),
                pl.BlockSpec((ext, LANES), fix),
                pl.BlockSpec((ext, LANES), fix),
                pl.BlockSpec((HALO, wide), col(0)),
                pl.BlockSpec((tok, wide), col(0)),
                pl.BlockSpec((HALO, wide), col(0)),
                pl.BlockSpec((pg, 2, lse.shape[2]), lambda i, s: (i, 0, 0)),
                pl.BlockSpec((pg, 2, lse.shape[2]), lambda i, s: (i, 0, 0)),
                pl.BlockSpec((tok, LANES), fix),
                pl.BlockSpec((tok, LANES), fix),
            ],
            out_specs=[pl.BlockSpec((tok, wide), col(0))] * 3,
            scratch_shapes=[
                pltpu.VMEM((pg, 2 * QB, 2 * LANES), BF),
                pltpu.VMEM((pg, 2 * QB, LANES), BF),
                pltpu.VMEM((ext, wide), BF),
                pltpu.VMEM((pg, ext, LANES), F32),
                pltpu.VMEM((pg, ext, LANES), F32),
            ],
        ),
        out_shape=[sh((tok, width), BF)] * 3,
        compiler_params=params(dimension_semantics=("arbitrary",)),
        cost_estimate=pl.CostEstimate(flops=80_000_000_000, bytes_accessed=20_000_000, transcendentals=0),
        name="attn_backward",
    )(scal, qkv, qkv, qkv, kt, qf, kf, gl, gc, gr, lse, dlt, cos, sin)


def gx_kernel(gq, gk, gv, w, x, gh2, g1, out, dg1):
    width = x.shape[1]
    gn = nt(gq[...], w[:, :width]) + nt(gk[...], w[:, width : 2 * width]) + nt(gv[...], w[:, 2 * width :])
    xf = x[...].astype(F32)
    mean = jnp.mean(xf, axis=-1, keepdims=True)
    cen = xf - mean
    r1 = lax.rsqrt(jnp.mean(cen * cen, axis=-1, keepdims=True) + EPS)
    nh = cen * r1

    @pl.when(pl.program_id(0) == 0)
    def _():
        dg1[...] = jnp.zeros_like(dg1)

    dg1[...] += jnp.sum(gn * nh, axis=0, keepdims=True)
    t = gn * g1[...]
    gx = gh2[...] + r1 * (t - jnp.mean(t, axis=-1, keepdims=True) - nh * jnp.mean(t * nh, axis=-1, keepdims=True))
    out[...] = gx.astype(BF)


def gx_call(gq, gk, gv, w, x, gh2, g1):
    tok, width = x.shape
    row = lambda i: (i, 0)
    fix = lambda i: (0, 0)
    rs = pl.BlockSpec((RB, width), row)
    return pl.pallas_call(
        gx_kernel,
        grid=(tok // RB,),
        in_specs=[rs, rs, rs, pl.BlockSpec(w.shape, fix), rs, rs, pl.BlockSpec(g1.shape, fix)],
        out_specs=[rs, pl.BlockSpec((1, width), fix)],
        out_shape=[jax.ShapeDtypeStruct((tok, width), BF), jax.ShapeDtypeStruct((1, width), F32)],
        compiler_params=params(dimension_semantics=("arbitrary",)),
        cost_estimate=pl.CostEstimate(flops=4_000_000_000, bytes_accessed=15_000_000, transcendentals=0),
        name="input_gradient",
    )(gq, gk, gv, w, x, gh2, g1)


def tn(a, b):
    return lax.dot_general(a, b, (((0,), (0,)), ((), ())), preferred_element_type=F32)


def on_device(tokens, cotangent, lengths, dealing, offsets, attn_gain, qkv_weight, out_weight,
              mlp_gain, in_weight, down_weight, *, n_replica, n_group):
    x, gy = tokens[0], cotangent[0]
    tok, width = x.shape
    n_qb = (tok + 2 * HALO) // QB
    replica = lax.axis_index("replica")
    right = [(i, i + 1) for i in range(n_replica - 1)]
    left = [(i + 1, i) for i in range(n_replica - 1)]

    gather = lambda a: lax.all_gather(a.astype(BF), "group", axis=0, tiled=True)
    x_l = lax.ppermute(x[tok - HALO :], "replica", right)
    x_r = lax.ppermute(x[:HALO], "replica", left)
    w_qkv = gather(qkv_weight)
    gains = lax.all_gather(jnp.stack([attn_gain, mlp_gain]).astype(BF), "group", axis=1, tiled=True).astype(F32)
    w_o, w_i, w_d = gather(out_weight), gather(in_weight), gather(down_weight)
    g1, g2 = gains[0:1], gains[1:2]

    seg, pos, scal = plan(lengths[0], replica, n_replica, tok)
    qf, kf = features(seg)
    cos, sin = rope_tables(pos)

    qkv, kt, vt, n1 = qkv_call(scal, x_l, x, x_r, w_qkv, g1, cos, sin, n_qb)
    o, lse = fwd_call(scal, qkv, vt, qf, kf, tok, width, n_qb, 2)
    out, m, gu, n2, gh2, gh2b, go, dlt, dg2 = mid_call(x, o, gy, w_o, w_i, w_d, g2)

    go_l = lax.ppermute(go[tok - HALO :], "replica", right)
    go_r = lax.ppermute(go[:HALO], "replica", left)
    pairs = width // LANES
    stats = jnp.concatenate([lse, dlt[: 2 * pairs].reshape(pairs, 2, tok)], axis=0)
    st_l = lax.ppermute(stats[:, :, tok - HALO :], "replica", right)
    st_r = lax.ppermute(stats[:, :, :HALO], "replica", left)
    st = jnp.concatenate([st_l, stats, st_r], axis=2)

    d_down = tn(m, gy)
    d_in = tn(n2, gu)
    d_out = tn(o, gh2b)

    co, si = cos[HALO : HALO + tok], sin[HALO : HALO + tok]
    gq, gk, gv = bwd_call(scal, qkv, kt, qf, kf, go_l, go, go_r, st[:pairs], st[pairs:], co, si, tok, width, n_qb, 2)
    d_qkv = jnp.concatenate([tn(n1, gq), tn(n1, gk), tn(n1, gv)], axis=1)
    gx, dg1 = gx_call(gq, gk, gv, w_qkv, x, gh2, g1)

    def reduce(a):
        s = lax.psum_scatter(a.astype(BF), "group", scatter_dimension=0, tiled=True)
        return lax.psum(s, "replica").astype(F32)

    dg = jnp.concatenate([dg1, dg2], axis=0).T
    dgs = reduce(dg)
    return (out[None], gx[None], dgs[:, 0], reduce(d_qkv), reduce(d_out), dgs[:, 1], reduce(d_in), reduce(d_down))


def solution(mesh):
    body = functools.partial(on_device, n_replica=mesh.shape["replica"], n_group=mesh.shape["group"])
    return jax.shard_map(
        body,
        mesh=mesh,
        in_specs=(
            P("group", "replica", None),
            P("group", "replica", None),
            P("group", None),
            P("group", None),
            P("group", None, None),
            P("group"),
            P("group", None),
            P("group", None),
            P("group"),
            P("group", None),
            P("group", None),
        ),
        out_specs=(
            P("group", "replica", None),
            P("group", "replica", None),
            P("group"),
            P("group", None),
            P("group", None),
            P("group"),
            P("group", None),
            P("group", None),
        ),
        check_vma=False,
    )
```

time: 1030 us -> 632 us (0.61)
  matrix products: 222 us -> 23 us
  waiting for transfers between devices: 511 us -> 325 us
  Pallas kernels: 0 us -> 175 us
  other arithmetic: 122 us -> 19.5 us
  local copies, waits for them, and re-layouts: 113 us -> 27.4 us
  starting transfers between devices: 0.53 us -> 15 us
    all_gather x8 -> x4, waiting for transfers between devices: 423 us -> 65 us  [on_device(): gather = lambda a: lax.all_gather(a.astype(BF), 'group', axis=0, tiled=True)]
    dot_general x23 -> x6, matrix products: 207 us -> 23 us  [tn(): lax.dot_general(a, b, (((0,), (0,)), ((), ())), preferred_element_type=F32)]
    pallas_call x0 -> x5, Pallas kernels: none -> 175 us  [the longest x1 73 us: bwd_call(): pl.pallas_call(functools.partial(bwd_kernel, pg, n_qb, tok), grid_spec=pl...]
    unnamed x13 -> x12, waiting for transfers between devices: 1.54 us -> 86.6 us
    reduce_scatter x4 -> x3, waiting for transfers between devices: 60.8 us -> 115 us  [reduce(): s = lax.psum_scatter(a.astype(BF), 'group', scatter_dimension=0, tiled=True)]
    convert_element_type x21 -> x12, other arithmetic: 63.7 us -> 11 us  [the longest x4 5.08 us: on_device(): gather = lambda a: lax.all_gather(a.astype(BF), 'group', axis=0, tiled=True)]
    gather x8 -> x0, local copies, waits for them, and re-layouts: 49.9 us -> none  [pick_rows(): taken = jnp.take(piece[0], jnp.clip(index_map, 0, piece_rows - 1), axis=0)]
    sub x2 -> x0, other arithmetic: 33.6 us -> none  [the longest x1 33.6 us: on_device(): exponent = jnp.exp(masked - row_top)]
  transfers between devices with their start and end apart: 13 -> 16, of which waited for: 11 -> 8; matrix products, arithmetic and copies ran while one was open for 36% -> 7% of each run, Pallas kernels for 0% -> 12%
where the time goes in v1:
time: 632 us; the launch traced here: 628 us
  waiting for transfers between devices  325 us (51%)
  Pallas kernels  175 us (28%)
  local copies, waits for them, and re-layouts  27.4 us (4%)
  blocking collectives  25.8 us (4%)
  matrix products  23 us (4%)
  other arithmetic  19.5 us (3%)
  between operations  17.2 us (3%)
  starting transfers between devices  15 us (2%)
    reduce_scatter x3, waiting for transfers between devices, reduce(): s = lax.psum_scatter(a.astype(BF), 'group', scatter_dimension=0, tiled=True)  115 us
    unnamed x12, waiting for transfers between devices  86.6 us
    pallas_call x1, Pallas kernels, bwd_call(): pl.pallas_call(functools.partial(bwd_kernel, pg, n_qb, tok), grid_spec=pl...  73 us
    all_gather x4, waiting for transfers between devices, on_device(): gather = lambda a: lax.all_gather(a.astype(BF), 'group', axis=0, tiled=True)  65 us
    psum x1, waiting for transfers between devices, reduce(): return lax.psum(s, 'replica').astype(F32)  57.4 us
    pallas_call x1, Pallas kernels, fwd_call(): pl.pallas_call(functools.partial(fwd_kernel, pg, n_qb, tok), grid_spec=pl...  45.1 us
    pallas_call x1, Pallas kernels, mid_call(): pl.pallas_call(mid_kernel, grid=(tok // RB,), in_specs=[rs(width), rs(wid...  27.8 us
    dot_general x6, matrix products, tn(): lax.dot_general(a, b, (((0,), (0,)), ((), ())), preferred_element_type=F32)  23 us
  transfers between devices with their start and end apart: 16, of which 8 were waited for; matrix products, arithmetic and copies ran while one was open for 7% of the time, Pallas kernels for 12%

profile of v1, /device:TPU:0, one launch (start us, length us, event | category | flops | bytes accessed | tf_op | source)
XLA Modules:
  0.0 627.6 jit_solution(992929569212683802)
XLA Ops:
  7.2 2.5 convert_element_type.82
  11.9 1.5 slice_bitcast_fusion
  14.8 4.3 collective-permute-start
  24.1 9.5 %all-gather = bf16[4,192,2]{1,2,0:T(2,128)(2,1)S(1)} all-gather(bf16[1,192,2]{1,2,0:T(2,128)(2,1)S(1)} %maximum_bitcast_fusion.1), channel_id=1, replica_groups=mesh['replica'=8,'group'=4] {'group'}, dimensions={0}, use_global_device_ids=true | all-gather | bytes 3840 | tf_op jit(solution)/shard_map/all_gather | solution.py:526
  34.5 2.1 select_convert_fusion
  37.8 6.6 %fusion = (f32[2816,128]{1,0:T(8,128)}, f32[2816,128]{1,0:T(8,128)}) fusion(f32[128]{0:T(128)S(1)} %get-tuple-element.124, f32[128]{0:T(128)S(1)} %get-tuple-element.125, f32[2816]{0:T(1024)S(1)} %get-tuple-element.119), kind=kLoop, calls=%fused_computation.9 | loop fusion | flops 720896 | bytes 2895872 | tf_op jit(solution)/shard_map/mul | solution.py:98
  44.4 16.0 %all-gather.6.cloned.1.call-done.w = bf16[768,2304]{1,0:T(8,128)(2,1)} async-done(((bf16[192,2304]{1,0:T(8,128)(2,1)}), bf16[768,2304]{1,0:T(8,128)(2,1)}) %all-gather.6.cloned.1.call-update) | async-done | bytes 3538960 | tf_op jit(solution)/shard_map/all_gather | solution.py:522
  60.4 19.4 %qkv.1 = (bf16[2816,2304]{1,0:T(8,128)(2,1)}, bf16[768,2816]{1,0:T(8,128)(2,1)}, bf16[768,2816]{1,0:T(8,128)(2,1)}, bf16[1024,768]{1,0:T(8,128)(2,1)}) custom-call(s32[53]{0:T(128)} %concatenate.17.scal, bf16[768,768]{1,0:T(8,128)(2,1)} %collective-permute-done.xl, bf16[1024,768]{1,0:T(8,128)(2,1)} %bitcast.48, bf16[768,768]{1,0:T(8,128)(2,1)} %copy-done.9, ...), custom_call_target="tpu_custom_call" | custom-call | flops 7077888000 | bytes 30000000 | tf_op jit(solution)/shard_map/qkv/pallas_call | solution.py:157
  79.9 45.1 %attn_forward.1 = (bf16[1024,768]{1,0:T(8,128)(2,1)}, f32[6,2,1024]{2,1,0:T(2,128)}) custom-call(s32[53]{0:T(128)} %concatenate.17.scal, bf16[2816,2304]{1,0:T(8,128)(2,1)} %get-tuple-element.28.q.k.v, bf16[2816,2304]{1,0:T(8,128)(2,1)} %get-tuple-element.28.q.k.v, bf16[768,2816]{1,0:T(8,128)(2,1)} %get-tuple-element.29.vt, ...), custom_call_target="tpu_custom_call" | custom-call | flops 30000001024 | bytes 15000000 | tf_op jit(solution)/shard_map/attn_forward/pallas_call | solution.py:257
  125.8 49.0 %all-gather.10.cloned.1.call-done.wi = bf16[768,2304]{1,0:T(8,128)(2,1)} async-done(((bf16[192,2304]{1,0:T(8,128)(2,1)}), bf16[768,2304]{1,0:T(8,128)(2,1)}) %all-gather.10.cloned.1.call-update) | async-done | bytes 3538960 | tf_op jit(solution)/shard_map/all_gather | solution.py:522
  174.8 27.8 %middle.1 = (bf16[1024,768]{1,0:T(8,128)(2,1)}, bf16[1024,1152]{1,0:T(8,128)(2,1)}, bf16[1024,2304]{1,0:T(8,128)(2,1)}, bf16[1024,768]{1,0:T(8,128)(2,1)}, f32[1...) custom-call(bf16[1024,768]{1,0:T(8,128)(2,1)} %bitcast.49, ...), custom_call_target="tpu_custom_call" | custom-call | flops 25999998976 | bytes 30000000 | tf_op jit(solution)/shard_map/middle/pallas_call | solution.py:348
  203.4 1.8 fusion.18
  206.5 3.1 collective-permute-start.2
  209.7 2.9 collective-permute-start.4
  214.1 1.9 slice.91.sin
  216.0 1.9 slice.90.cos
  220.1 73.0 %attn_backward.1 = (bf16[1024,768]{1,0:T(8,128)(2,1)}, bf16[1024,768]{1,0:T(8,128)(2,1)}, bf16[1024,768]{1,0:T(8,128)(2,1)}) custom-call(s32[53]{0:T(128)} %concatenate.17.scal, bf16[2816,2304]{1,0:T(8,128)(2,1)} %get-tuple-element.28.q.k.v, bf16[2816,2304]{1,0:T(8,128)(2,1)} %get-tuple-element.28.q.k.v, bf16[2816,2304]{1,0:T(8,128)(2,1)} %get-tuple-element.28.q.k.v, ...), custom_call_target="tpu_custom_call" | custom-call | flops 80000000000 | bytes 20000000 | tf_op jit(solution)/shard_map/attn_backward/pallas_call | solution.py:437
  293.1 3.5 convolution_convert_fusion.3
  300.0 3.9 copy.29
  305.3 4.0 convolution_convert_fusion.2
  309.4 4.9 convolution_convert_fusion.1
  315.7 7.6 %convolution_convert_fusion = bf16[768,2304]{1,0:T(8,128)(2,1)} fusion(bf16[1024,768]{1,0:T(8,128)(2,1)S(1)} %copy-done.20, bf16[1024,2304]{1,0:T(8,128)(2,1)} %get-tuple-element.46), kind=kOutput, calls=%fused_computation | convolution fusion | flops 3625648128 | bytes 9830400 | tf_op jit(solution)/shard_map/dot_general | solution.py:510
  324.0 9.9 %input_gradient.1 = (bf16[1024,768]{1,0:T(8,128)(2,1)}, f32[1,768]{1,0:T(1,128)}) custom-call(bf16[1024,768]{1,0:T(8,128)(2,1)} %get-tuple-element.36.gq, bf16[1024,768]{1,0:T(8,128)(2,1)} %get-tuple-element.37.gk, bf16[1024,768]{1,0:T(8,128)(2,1)} %get-tuple-element.38.gv, bf16[768,2304]{1,0:T(8,128)(2,1)} %all-gather.6.cloned.1.call-done.w, ...), custom_call_target="tpu_custom_call" | custom-call | flops 4000000000 | bytes 15000000 | tf_op jit(solution)/shard_map/input_gradient/pallas_call | solution.py:497
  335.6 59.1 %reduce-scatter.18.cloned.1.call-done = bf16[192,2304]{1,0:T(8,128)(2,1)} async-done(((bf16[768,2304]{1,0:T(8,128)(2,1)}), bf16[192,2304]{1,0:T(8,128)(2,1)}) %reduce-scatter.18.cloned.1.call-update) | async-done | bytes 884752
  394.7 2.3 copy.30
  397.0 29.0 %reduce-scatter.10.cloned.1.call-done = bf16[192,768]{1,0:T(8,128)(2,1)} async-done(((bf16[768,768]{1,0:T(8,128)(2,1)}), bf16[192,768]{1,0:T(8,128)(2,1)}) %reduce-scatter.10.cloned.1.call-update) | async-done | bytes 294928 | tf_op jit(solution)/shard_map/reduce_scatter | solution.py:556
  426.0 36.1 %reduce-scatter.14.cloned.1.call-done = bf16[288,768]{1,0:T(8,128)(2,1)} async-done(((bf16[1152,768]{1,0:T(8,128)(2,1)}), bf16[288,768]{1,0:T(8,128)(2,1)}) %reduce-scatter.14.cloned.1.call-update) | async-done | bytes 442384 | tf_op jit(solution)/shard_map/reduce_scatter | solution.py:556
  462.2 50.3 %reduce-scatter.12.cloned.1.call-done = bf16[192,2304]{1,0:T(8,128)(2,1)} async-done(((bf16[768,2304]{1,0:T(8,128)(2,1)}), bf16[192,2304]{1,0:T(8,128)(2,1)}) %reduce-scatter.12.cloned.1.call-update) | async-done | bytes 884752 | tf_op jit(solution)/shard_map/reduce_scatter | solution.py:556
  512.5 27.4 %reduce-scatter.16.cloned.1.call-done = bf16[192,2]{1,0:T(8,128)(2,1)} async-done(((bf16[768,2]{1,0:T(8,128)(2,1)}), bf16[192,2]{1,0:T(8,128)(2,1)}) %reduce-scatter.16.cloned.1.call-update) | async-done | bytes 784
  540.7 16.3 %psum.35 = bf16[192,2]{0,1:T(2,128)(2,1)S(1)} all-reduce(bf16[192,2]{0,1:T(2,128)(2,1)S(1)} %copy.28), channel_id=1, replica_groups=mesh['replica'=8,'group'=4] {'replica'}, use_global_device_ids=true, to_apply=%region_8.9 | all-reduce | flops 384 | bytes 1536 | tf_op jit(solution)/shard_map/psum | solution.py:557
  557.6 57.4 %all-reduce.3.cloned.1.call-done = (bf16[192,2304]{0,1:T(8,128)(2,1)}, bf16[192,768]{1,0:T(8,128)(2,1)}, bf16[192,2304]{1,0:T(8,128)(2,1)}, bf16[288,768]{1,0:T(8,128)(2,1)}) async-done(((bf16[192,2304]{0,1:T(8,128)(2,1)}, bf16[192,768]{1,0:T(8,128)(2,1)}, bf16[192,2304]{1,0:T(8,128)(2,1)}, bf16[288,768]{1,0:T(8,128)(2,1)}), (bf16[192,2304]{0,1:T(8,128)(2,1)}, bf16[192,768]{1,0:T(8,128)(2,1)}, ...) | async-done | bytes 2506768 | tf_op jit(solution)/shard_map/psum | solution.py:557
  615.1 2.6 copy.26
  (120 shorter events, 27.6 us)
Async XLA Ops:
  7.2 2.7 copy-start.4
  7.2 53.3 %all-gather.6.cloned.1.call-start = ((), (), s32[]{:S(2)}) async-start(), calls=%async_computation.5 | async-start | bytes 4423680 | tf_op jit(solution)/shard_map/all_gather | solution.py:522
  9.8 2.1 copy-start
  9.8 116.0 %all-gather.8.cloned.1.call-start = ((), (), s32[]{:S(2)}) async-start(), calls=%async_computation.6 | async-start | bytes 1474560 | tf_op jit(solution)/shard_map/all_gather | solution.py:522
  10.6 115.2 %all-gather.12.cloned.1.call-start = ((), (), s32[]{:S(2)}) async-start(), calls=%async_computation.8 | async-start | bytes 2211840 | tf_op jit(solution)/shard_map/all_gather | solution.py:522
  11.9 7.2 %copy-start.1 = (f32[192,2304]{1,0:T(8,128)S(1)}, f32[192,2304]{1,0:T(8,128)}, u32[]{:S(2)}) copy-start(f32[192,2304]{1,0:T(8,128)} %param.19) | copy-start | bytes 5308420
  11.9 162.9 %all-gather.10.cloned.1.call-start = ((), (), s32[]{:S(2)}) async-start(), calls=%async_computation.7 | async-start | bytes 4423680 | tf_op jit(solution)/shard_map/all_gather | solution.py:522
  13.5 30.9 %collective-permute-start.1 = (bf16[768,768]{1,0:T(8,128)(2,1)}, bf16[768,768]{1,0:T(8,128)(2,1)S(1)}, u32[]{:S(2)}, u32[]{:S(2)}) collective-permute-start(bf16[768,768]{1,0:T(8,128)(2,1)} %get-tuple-element.100), channel_id=1, source_target_pairs={{4,0},{8,4},{12,8},{16,12},{20,16},{24,20},{28,24},{5,1},{9,5},{13... | collective-permute-start | bytes 3538952 | tf_op jit(solution)/shard_map/ppermute | solution.py:524
  14.8 5.4 copy-start.14
  14.8 5.5 copy-start.15
  14.8 7.7 %copy-start.12 = (f32[192]{0:T(256)S(1)}, f32[192]{0:T(256)}, u32[]{:S(2)}) copy-start(f32[192]{0:T(256)} %param.15) | copy-start | bytes 2308
  14.8 7.7 %copy-start.13 = (f32[192]{0:T(256)S(1)}, f32[192]{0:T(256)}, u32[]{:S(2)}) copy-start(f32[192]{0:T(256)} %param.18) | copy-start | bytes 2308
  14.8 29.6 %collective-permute-start = (bf16[768,768]{1,0:T(8,128)(2,1)}, bf16[768,768]{1,0:T(8,128)(2,1)}, u32[]{:S(2)}, u32[]{:S(2)}) collective-permute-start(bf16[768,768]{1,0:T(8,128)(2,1)} %get-tuple-element.101), channel_id=1, source_target_pairs={{0,4},{4,8},{8,12},{12,16},{16,20},{20,24},{24,28},{1,5},{5,9},{9,... | collective-permute-start | bytes 3538952 | tf_op jit(solution)/shard_map/ppermute | solution.py:523
  20.1 374.6 %reduce-scatter.18.cloned.1.call-start = ((), (), s32[]{:S(2)}) async-start(), calls=%async_computation.13 | async-start | bytes 4423680
  44.4 16.0 %copy-start.9 = (bf16[768,768]{1,0:T(8,128)(2,1)}, bf16[768,768]{1,0:T(8,128)(2,1)S(1)}, u32[]{:S(2)}) copy-start(bf16[768,768]{1,0:T(8,128)(2,1)S(1)} %collective-permute-done.1.xr) | copy-start | bytes 3538948
  205.2 13.5 %collective-permute-start.3 = (bf16[768,768]{1,0:T(8,128)(2,1)S(1)}, bf16[768,768]{1,0:T(8,128)(2,1)S(1)}, u32[]{:S(2)}, u32[]{:S(2)}) collective-permute-start(bf16[768,768]{1,0:T(8,128)(2,1)S(1)} %get-tuple-element.98), channel_id=1, source_target_pairs={{4,0},{8,4},{12,8},{16,12},{20,16},{24,20},{28,24},{5,1},{9,5},{13... | collective-permute-start | bytes 3538952 | tf_op jit(solution)/shard_map/ppermute | solution.py:539
  206.5 12.2 %collective-permute-start.2 = (bf16[768,768]{1,0:T(8,128)(2,1)S(1)}, bf16[768,768]{1,0:T(8,128)(2,1)S(1)}, u32[]{:S(2)}, u32[]{:S(2)}) collective-permute-start(bf16[768,768]{1,0:T(8,128)(2,1)S(1)} %get-tuple-element.99), channel_id=1, source_target_pairs={{0,4},{4,8},{8,12},{12,16},{16,20},{20,24},{24,28},{1,5},{5,9},{9,... | collective-permute-start | bytes 3538952 | tf_op jit(solution)/shard_map/ppermute | solution.py:538
  209.7 8.2 %collective-permute-start.4 = (f32[12,2,768]{2,1,0:T(2,128)S(1)}, f32[12,2,768]{2,1,0:T(2,128)S(1)}, u32[]{:S(2)}, u32[]{:S(2)}) collective-permute-start(f32[12,2,768]{2,1,0:T(2,128)S(1)} %get-tuple-element.104), channel_id=1, source_target_pairs={{0,4},{4,8},{8,12},{12,16},{16,20},{20,24},{24,28},{1,5},{5,9},{9,... | collective-permute-start | bytes 221192 | tf_op jit(solution)/shard_map/ppermute | solution.py:542
  212.6 5.2 collective-permute-start.5
  293.0 3.5 copy-start.17
  293.0 3.5 copy-start.19
  296.5 1.5 copy-start.16
  303.9 1.4 copy-start.18
  303.9 122.1 %reduce-scatter.10.cloned.1.call-start = ((), (), s32[]{:S(2)}) async-start(), calls=%async_computation.9 | async-start | bytes 1474560 | tf_op jit(solution)/shard_map/reduce_scatter | solution.py:556
  305.3 4.1 copy-start.8
  309.3 152.8 %reduce-scatter.14.cloned.1.call-start = ((), (), s32[]{:S(2)}) async-start(), calls=%async_computation.11 | async-start | bytes 2211840 | tf_op jit(solution)/shard_map/reduce_scatter | solution.py:556
  314.3 198.1 %reduce-scatter.12.cloned.1.call-start = ((), (), s32[]{:S(2)}) async-start(), calls=%async_computation.10 | async-start | bytes 4423680 | tf_op jit(solution)/shard_map/reduce_scatter | solution.py:556
  323.4 216.5 %reduce-scatter.16.cloned.1.call-start = ((), (), s32[]{:S(2)}) async-start(), calls=%async_computation.12 | async-start | bytes 245760
  335.6 279.5 %all-reduce.3.cloned.1.call-start = ((), (), s32[]{:S(2)}) async-start(), calls=%async_computation.14 | async-start | bytes 5603328 | tf_op jit(solution)/shard_map/psum | solution.py:557
  615.0 2.6 copy-start.6
  615.0 3.4 copy-start.5
  617.6 1.8 copy-start.3
  (5 other events, 5.8 us)
Sparse Core Ops, SparseCore 0:
  10.4 49.9 all-gather.5
  62.3 27.7 all-gather.7
  92.5 32.7 all-gather.11
  127.6 47.1 all-gather.9
  304.1 90.5 reduce-scatter.17
  397.5 28.5 reduce-scatter.9
  429.6 32.4 reduce-scatter.13
  465.2 47.1 reduce-scatter.11
  515.8 23.9 reduce-scatter.15
  542.9 72.0 all-reduce.2

commit v2 on v1

v2 whole, which is shorter than its diff:
```python
import functools
import math

import jax
import jax.numpy as jnp
from jax import lax
from jax.experimental import pallas as pl
from jax.experimental.pallas import tpu as pltpu
from jax.sharding import PartitionSpec as P

HEADS = 12
HEAD_DIM = 64
LANES = 128
HALO = 768
RB = 256
QB = 128
KB = 256
EPS = 1e-05
BIG = -1e30
ROPE_BASE = 160000.0
LOG2E = 1.4426950408889634
LN2 = 0.6931471805599453
BF = jnp.bfloat16
F32 = jnp.float32


def nt(a, b):
    return lax.dot_general(a, b, (((1,), (1,)), ((), ())), preferred_element_type=F32)


def nn(a, b):
    return lax.dot_general(a, b, (((1,), (0,)), ((), ())), preferred_element_type=F32)


def partner(x):
    lane = lax.broadcasted_iota(jnp.int32, x.shape, 1) % HEAD_DIM
    return jnp.where(lane < HEAD_DIM // 2, pltpu.roll(x, 96, 1), pltpu.roll(x, 32, 1))


def half_of(rows):
    return -(-rows // 32) * 16


def row_of(place, rows):
    return pl.multiple_of((place // 2) * rows + (place % 2) * (rows - half_of(rows)), 16)


def params(mib, **kw):
    return pltpu.CompilerParams(vmem_limit_bytes=mib * 1024 * 1024, **kw)


class Sizes:
    def __init__(self, tok, width):
        self.tok, self.width = tok, width
        self.ext = tok + 2 * HALO + RB
        self.n_qb = (tok + 2 * HALO) // QB
        self.own_qb, self.own_lo = tok // QB, HALO // QB
        self.own_hi = self.own_lo + self.own_qb
        tiles = -(-(QB + 2 * HALO + QB) // KB)
        self.cap_f = self.own_qb * tiles + 2
        self.cap_b = self.own_qb * tiles + 2 * self.own_lo * -(-(HALO + QB) // KB) + 2
        self.k_lo, self.k_n = 0, self.n_qb
        self.q_lo, self.q_hi = 2 * self.n_qb, 2 * self.n_qb + 1
        self.need_lo, self.need_hi = 2 * self.n_qb + 2, 2 * self.n_qb + 3
        self.blocks = self.ext // RB
        self.fwd_q = self.need_hi + 1
        self.fwd_k, self.fwd_n = self.fwd_q + self.cap_f, self.fwd_q + 2 * self.cap_f
        self.bwd_q = self.fwd_n + 1
        self.bwd_k, self.bwd_n = self.bwd_q + self.cap_b, self.bwd_q + 2 * self.cap_b
        self.places = self.bwd_n + 1


def plan_kernel(sz, n_replica, n_group, where, lengths, scal, qf, kf, cos, sin, starts, seg_buf, pos_buf):
    n_seq = lengths.shape[1]
    total = n_replica * sz.tok
    replica, group = where[0], where[1]
    base = replica * sz.tok - HALO
    at = jnp.int32(0)
    for j in range(n_seq):
        starts[j] = at
        at = at + lengths[0, j]
    starts[n_seq] = at

    def first_of(g):
        return lax.fori_loop(0, n_seq, lambda j, f: jnp.where(g >= starts[j], starts[j], f), jnp.int32(0))

    def last_of(g):
        return lax.fori_loop(0, n_seq, lambda j, l: jnp.where(g >= starts[j], starts[j + 1], l), jnp.int32(total))

    own_a, own_b = base + HALO, base + HALO + sz.tok - 1
    first_a, last_a = first_of(own_a) - base, last_of(own_a) - base
    first_b, last_b = first_of(own_b) - base, last_of(own_b) - base
    q_lo, q_hi = first_a // QB, (last_b + QB - 1) // QB
    scal[sz.q_lo], scal[sz.q_hi] = q_lo, q_hi

    def block(i, _):
        e = i * QB
        left, right = i < sz.own_lo, i >= sz.own_hi
        lo = jnp.where(left, HALO, jnp.where(right, first_b, first_of(base + e) - base)) // QB
        hi = jnp.where(left, last_a, jnp.where(right, HALO + sz.tok, last_of(base + e + QB - 1) - base))
        n = (hi - lo * QB + (KB - 1)) // KB
        scal[sz.k_lo + i] = lo
        scal[sz.k_n + i] = jnp.where((i >= q_lo) & (i < q_hi), n, 0)
        return 0

    lax.fori_loop(0, sz.n_qb, block, 0)
    scal[sz.need_lo], scal[sz.need_hi] = first_a // RB, (last_b + KB - 1 + RB - 1) // RB

    def tiles(first, count, at_q, at_k, at_n):
        def of_block(i, c):
            lo, n = scal[sz.k_lo + i], scal[sz.k_n + i]

            def one(t, c):
                scal[at_q + c] = i - first
                scal[at_k + c] = lo + t * (KB // QB)
                return c + 1

            return lax.fori_loop(0, n, one, c)

        c = lax.fori_loop(first, first + count, of_block, jnp.int32(0))
        scal[at_n] = c
        for extra in range(2):
            scal[at_q + c + extra] = jnp.int32(count)
            scal[at_k + c + extra] = jnp.int32(sz.own_lo)

    tiles(sz.own_lo, sz.own_qb, sz.fwd_q, sz.fwd_k, sz.fwd_n)
    tiles(0, sz.n_qb, sz.bwd_q, sz.bwd_k, sz.bwd_n)
    core = replica % 2
    for k in range(n_group):
        for h in range(2):
            scal[sz.places + 2 * k + h] = 2 * (group ^ k) + (core ^ h)

    half = HEAD_DIM // 2
    blocks = sz.ext // QB
    g = base + QB * lax.broadcasted_iota(jnp.int32, (blocks, QB), 0) + lax.broadcasted_iota(jnp.int32, (blocks, QB), 1)
    seg = jnp.full((blocks, QB), -1, jnp.int32)
    first = jnp.zeros((blocks, QB), jnp.int32)
    for j in range(n_seq):
        hit = g >= starts[j]
        seg = jnp.where(hit, j, seg)
        first = jnp.where(hit, starts[j], first)
    seg_buf[...] = jnp.where(g >= total, n_seq, seg) & 15
    pos_buf[...] = jnp.maximum(g - first, 0).astype(F32)
    freq = jnp.exp(lax.broadcasted_iota(jnp.int32, (half, QB), 0).astype(F32) * (-2.0 / HEAD_DIM * math.log(ROPE_BASE)))

    def rows(b, _):
        r0 = pl.multiple_of(b * QB, QB)
        hot = (seg_buf[pl.ds(b, 1), :] == lax.broadcasted_iota(jnp.int32, (LANES, QB), 0)).astype(F32).T
        qf[pl.ds(r0, QB), :] = (hot * BIG).astype(BF)
        lane = lax.broadcasted_iota(jnp.int32, (QB, LANES), 1)
        kf[pl.ds(r0, QB), :] = jnp.where(lane < 16, 1.0 - hot, 0.0).astype(BF)
        ang = freq * pos_buf[pl.ds(b, 1), :]
        co, si = jnp.cos(ang), jnp.sin(ang)
        cos[pl.ds(r0, QB), :] = jnp.concatenate([co] * 4, axis=0).T
        sin[pl.ds(r0, QB), :] = jnp.concatenate([-si, si, -si, si], axis=0).T
        return 0

    lax.fori_loop(0, blocks, rows, 0)


def plan_call(sz, n_replica, n_group, where, lengths):
    sh = jax.ShapeDtypeStruct
    smem = pl.BlockSpec(memory_space=pltpu.SMEM)
    vmem = pl.BlockSpec(memory_space=pltpu.VMEM)
    n_seq = lengths.shape[1]
    return pl.pallas_call(
        functools.partial(plan_kernel, sz, n_replica, n_group),
        in_specs=[smem, smem],
        out_specs=[smem] + [vmem] * 4,
        out_shape=[sh((sz.places + 2 * n_group,), jnp.int32)] + [sh((sz.ext, LANES), BF)] * 2 + [sh((sz.ext, LANES), F32)] * 2,
        scratch_shapes=[pltpu.SMEM((n_seq + 1,), jnp.int32), pltpu.VMEM((sz.ext // QB, QB), jnp.int32), pltpu.VMEM((sz.ext // QB, QB), F32)],
        compiler_params=params(60),
        cost_estimate=pl.CostEstimate(flops=10_000_000_000, bytes_accessed=5_000_000, transcendentals=0),
        name="plan",
    )(where, lengths)


def fetch_qkv(place, pieces, w, sem):
    copies = []
    shard = w.shape[0] // (len(pieces) // 2)
    for t, piece in enumerate(pieces):
        copies.append(pltpu.make_async_copy(piece, w.at[pl.ds(row_of(place(t), shard), piece.shape[0]), :], sem.at[t]))
    return copies


def qkv_kernel(sz, n_pieces, scal, xl, xc, xr, *rest):
    pieces, (g1, cos, sin, qkv, kt, vt, n1t, w, sem) = rest[:n_pieces], rest[n_pieces:]
    i = pl.program_id(0)
    left_b, own_b = HALO // RB, sz.tok // RB
    own = (i >= left_b) & (i < left_b + own_b)

    @pl.when(i == 0)
    def _():
        copies = fetch_qkv(lambda t: scal[sz.places + t], pieces, w, sem)
        for c in copies:
            c.start()
        for c in copies:
            c.wait()

    @pl.when((i >= scal[sz.need_lo]) & (i < scal[sz.need_hi]))
    def _():
        x = jnp.where(i < left_b, xl[...], jnp.where(i < left_b + own_b, xc[...], xr[...])).astype(F32)
        mean = jnp.mean(x, axis=-1, keepdims=True)
        cen = x - mean
        var = jnp.mean(cen * cen, axis=-1, keepdims=True)
        n1 = (cen * lax.rsqrt(var + EPS) * g1[...]).astype(BF)

        @pl.when(own)
        def _():
            n1t[...] = n1.T

        width = n1.shape[1]
        co, si = cos[...], sin[...]
        sc = HEAD_DIM ** -0.5 * LOG2E
        cq, sq = co * sc, si * sc
        for c in range(3 * width // 256):
            a = nn(n1, w[:, 256 * c : 256 * c + 256])
            part = 256 * c // width
            off = 256 * c - width * part
            if part < 2:
                cc, ss = (cq, sq) if part == 0 else (co, si)
                halves = []
                for h in range(2):
                    b = a[:, 128 * h : 128 * h + 128]
                    halves.append((b * cc + partner(b) * ss).astype(BF))
                r = jnp.concatenate(halves, axis=1)
            else:
                r = a.astype(BF)
            qkv[:, 256 * c : 256 * c + 256] = r
            if part == 1:
                kt[off : off + 256, :] = r.T
            if part == 2:
                vt[off : off + 256, :] = r.T


def qkv_call(sz, scal, xl, xc, xr, pieces, g1, cos, sin):
    tok, width, ext = sz.tok, sz.width, sz.ext
    own_b, lb = tok // RB, HALO // RB
    clampi = lambda lo, n: (lambda i, s: (jnp.clip(i - lo, 0, n - 1), 0))
    used = lambda i, s: jnp.clip(i, s[sz.need_lo], s[sz.need_hi] - 1)
    row = lambda i, s: (used(i, s), 0)
    fix = lambda i, s: (0, 0)
    col = lambda i, s: (0, used(i, s))
    sh = jax.ShapeDtypeStruct
    return pl.pallas_call(
        functools.partial(qkv_kernel, sz, len(pieces)),
        grid_spec=pltpu.PrefetchScalarGridSpec(
            num_scalar_prefetch=1,
            grid=(sz.blocks,),
            in_specs=[
                pl.BlockSpec((RB, width), clampi(0, lb)),
                pl.BlockSpec((RB, width), clampi(lb, own_b)),
                pl.BlockSpec((RB, width), clampi(lb + own_b, lb)),
                *[pl.BlockSpec(memory_space=pl.ANY)] * len(pieces),
                pl.BlockSpec((1, width), fix),
                pl.BlockSpec((RB, LANES), row),
                pl.BlockSpec((RB, LANES), row),
            ],
            out_specs=[
                pl.BlockSpec((RB, 3 * width), row),
                pl.BlockSpec((width, RB), col),
                pl.BlockSpec((width, RB), col),
                pl.BlockSpec((width, RB), lambda i, s: (0, jnp.clip(i - lb, 0, own_b - 1))),
            ],
            scratch_shapes=[pltpu.VMEM((width, 3 * width), BF), pltpu.SemaphoreType.DMA((len(pieces),))],
        ),
        out_shape=[sh((ext, 3 * width), BF), sh((width, ext), BF), sh((width, ext), BF), sh((width, tok), BF)],
        compiler_params=params(60, dimension_semantics=("arbitrary",)),
        cost_estimate=pl.CostEstimate(flops=14_000_000_000, bytes_accessed=30_000_000, transcendentals=0),
        name="qkv",
    )(scal, xl, xc, xr, *pieces, g1, cos, sin)


def split_heads(x):
    low = lax.broadcasted_iota(jnp.int32, x.shape, 1) < HEAD_DIM
    zero = jnp.zeros_like(x)
    return jnp.concatenate([jnp.where(low, x, zero), jnp.where(low, zero, x)], axis=0)


def lanes_of(p):
    return slice(LANES * p, LANES * p + LANES)


def fwd_kernel(sz, pg, scal, q, k, vt, qf, kf, out, out_t, lse, q2, buf_a, buf_b, acc, tops):
    nq = sz.own_qb
    ones = jnp.ones((16, KB), BF)
    for qi in range(nq):
        r0 = HALO + qi * QB
        fq = qf[r0 : r0 + QB, :]
        f2 = jnp.concatenate([fq, fq], axis=0)
        for p in range(pg):
            q2[qi, p] = jnp.concatenate([split_heads(q[r0 : r0 + QB, lanes_of(p)]), f2], axis=1)

    def zero(i, _):
        for p in range(pg):
            acc[i, p] = jnp.zeros((LANES + 16, 2 * QB), F32)
            tops[i, p] = jnp.zeros((8, 2 * QB), F32)
        return 0

    lax.fori_loop(0, nq + 1, zero, 0)

    def scores(qi, k0, p, fk):
        return nt(jnp.concatenate([k[pl.ds(k0, KB), lanes_of(p)], fk], axis=1), q2[qi, p])

    def mixed(k0, p, probs):
        va = jnp.concatenate([vt[lanes_of(p), pl.ds(k0, KB)], ones], axis=0)
        return nn(va, probs.astype(BF))

    def tile(i):
        return scal[sz.fwd_q + i], pl.multiple_of(scal[sz.fwd_k + i] * QB, QB)

    def score_tile(i, buf):
        qi, k0 = tile(i)
        qi = jnp.minimum(qi, nq - 1)
        fk = kf[pl.ds(k0, KB), :]
        for p in range(pg):
            buf[p] = scores(qi, k0, p, fk)

    def mix_tile(i, buf):
        qi, k0 = tile(i)
        for p in range(pg):
            acc[qi, p] += mixed(k0, p, jnp.exp2(buf[p]))

    score_tile(0, buf_a)

    def body(j, _):
        score_tile(2 * j + 1, buf_b)
        mix_tile(2 * j, buf_a)
        score_tile(2 * j + 2, buf_a)
        mix_tile(2 * j + 1, buf_b)
        return 0

    lax.fori_loop(0, (scal[sz.fwd_n] + 1) // 2, body, 0)

    low = high = acc[0, 0, LANES : LANES + 1, :]
    for qi in range(nq):
        for p in range(pg):
            total = acc[qi, p, LANES : LANES + 1, :]
            low, high = jnp.minimum(low, total), jnp.maximum(high, total)
    safe = (jnp.min(low) > 2.0 ** -60) & (jnp.max(high) < 2.0 ** 100)

    @pl.when(jnp.logical_not(safe))
    def _():
        lax.fori_loop(0, nq, zero, 0)

        def per_q(qi, _):
            lo, n = scal[sz.k_lo + sz.own_lo + qi], scal[sz.k_n + sz.own_lo + qi]
            for p in range(pg):
                def top(t, m):
                    k0 = pl.multiple_of(lo * QB + t * KB, QB)
                    return jnp.maximum(m, jnp.max(scores(qi, k0, p, kf[pl.ds(k0, KB), :]), axis=0, keepdims=True))

                m = lax.fori_loop(0, n, top, jnp.full((1, 2 * QB), BIG, F32))
                tops[qi, p] = jnp.broadcast_to(m, (8, 2 * QB))

                def add(t, _):
                    k0 = pl.multiple_of(lo * QB + t * KB, QB)
                    acc[qi, p] += mixed(k0, p, jnp.exp2(scores(qi, k0, p, kf[pl.ds(k0, KB), :]) - m))
                    return 0

                lax.fori_loop(0, n, add, 0)
            return 0

        lax.fori_loop(0, nq, per_q, 0)

    def finish(qi, _):
        o0 = pl.multiple_of(qi * QB, QB)
        for p in range(pg):
            a = acc[qi, p]
            total = a[LANES : LANES + 1, :]
            inv = 1.0 / total
            o_t = jnp.concatenate([a[:HEAD_DIM, :QB] * inv[:, :QB], a[HEAD_DIM:LANES, QB:] * inv[:, QB:]], axis=0).astype(BF)
            out_t[lanes_of(p), pl.ds(o0, QB)] = o_t
            out[pl.ds(o0, QB), lanes_of(p)] = o_t.T
            st = tops[qi, p, 0:1, :] + jnp.log2(total)
            lse[p, 0:1, pl.ds(o0, QB)] = st[:, :QB]
            lse[p, 1:2, pl.ds(o0, QB)] = st[:, QB:]
        return 0

    lax.fori_loop(0, nq, finish, 0)


def fwd_call(sz, scal, qkv, vt, qf, kf, pg):
    ext, tok, width = sz.ext, sz.tok, sz.width
    pairs = width // LANES
    steps = pairs // pg
    wide = LANES * pg
    col = lambda off: (lambda i, s: (0, off + i))
    fix = lambda i, s: (0, 0)
    sh = jax.ShapeDtypeStruct
    return pl.pallas_call(
        functools.partial(fwd_kernel, sz, pg),
        grid_spec=pltpu.PrefetchScalarGridSpec(
            num_scalar_prefetch=1,
            grid=(steps,),
            in_specs=[
                pl.BlockSpec((ext, wide), col(0)),
                pl.BlockSpec((ext, wide), col(steps)),
                pl.BlockSpec((wide, ext), lambda i, s: (i, 0)),
                pl.BlockSpec((ext, LANES), fix),
                pl.BlockSpec((ext, LANES), fix),
            ],
            out_specs=[
                pl.BlockSpec((tok, wide), col(0)),
                pl.BlockSpec((wide, tok), lambda i, s: (i, 0)),
                pl.BlockSpec((pg, 2, tok), lambda i, s: (i, 0, 0)),
            ],
            scratch_shapes=[
                pltpu.VMEM((sz.own_qb, pg, 2 * QB, 2 * LANES), BF),
                pltpu.VMEM((pg, KB, 2 * QB), F32),
                pltpu.VMEM((pg, KB, 2 * QB), F32),
                pltpu.VMEM((sz.own_qb + 1, pg, LANES + 16, 2 * QB), F32),
                pltpu.VMEM((sz.own_qb + 1, pg, 8, 2 * QB), F32),
            ],
        ),
        out_shape=[sh((tok, width), BF), sh((width, tok), BF), sh((pairs, 2, tok), F32)],
        compiler_params=params(60, dimension_semantics=("arbitrary",)),
        cost_estimate=pl.CostEstimate(flops=30_000_000_000, bytes_accessed=15_000_000, transcendentals=0),
        name="attn_forward",
    )(scal, qkv, qkv, vt, qf, kf)


def fetch_mlp(place, pieces, wo, wi, wd, sem, width):
    copies = []
    shards = len(pieces) // 2
    half, half_d = half_of(wo.shape[0] // shards), half_of(wd.shape[0] // shards)
    t_cols = wi.shape[1] // width
    for t, piece in enumerate(pieces):
        row0 = row_of(place(t), wo.shape[0] // shards)
        row_d = row_of(place(t), wd.shape[0] // shards)
        copies.append(pltpu.make_async_copy(piece.at[0:half, :], wo.at[pl.ds(row0, half), :], sem.at[t, 0]))
        for j in range(t_cols):
            copies.append(pltpu.make_async_copy(
                piece.at[half * (j + 1) : half * (j + 2), :],
                wi.at[pl.ds(row0, half), width * j : width * j + width], sem.at[t, j + 1]))
        lo = half * (t_cols + 1)
        copies.append(pltpu.make_async_copy(piece.at[lo : lo + half_d, :], wd.at[pl.ds(row_d, half_d), :], sem.at[t, t_cols + 1]))
    return copies


def mid_kernel(n_pieces, at, scal, *refs):
    pieces, refs = refs[:n_pieces], refs[n_pieces:]
    wo, wi, wd, sem = refs[-4:]

    @pl.when(pl.program_id(0) == 0)
    def _():
        copies = fetch_mlp(lambda t: scal[at + t], pieces, wo, wi, wd, sem, wo.shape[1])
        for c in copies:
            c.start()
        for c in copies:
            c.wait()

    x, o, gy, g2, ind = refs[:5]
    mid_body(x, o, gy, wo, wi, wd, g2, ind, *refs[5:-4])


def mid_body(x, o, gy, wo, wi, wd, g2, ind, out, mt_o, gu_o, n2t_o, gh2b_o, go_o, dlt):
    ff = wd.shape[0]
    h2 = x[...].astype(F32) + nn(o[...], wo[...])
    mean = jnp.mean(h2, axis=-1, keepdims=True)
    cen = h2 - mean
    r2 = lax.rsqrt(jnp.mean(cen * cen, axis=-1, keepdims=True) + EPS)
    nh = cen * r2
    g = g2[...]
    n2 = (nh * g).astype(BF)
    n2t_o[...] = n2.T
    gyb = gy[...]
    y = h2
    gn2 = jnp.zeros_like(h2)
    step = 384
    for c in range(ff // step):
        lo = c * step
        a = nn(n2, wi[:, lo : lo + step])
        b = nn(n2, wi[:, ff + lo : ff + lo + step])
        gm = nt(gyb, wd[lo : lo + step, :])
        half = 0.5 * (1.0 + lax.erf(a * (2.0 ** -0.5)))
        gel = a * half
        mm = (gel * b).astype(BF)
        mt_o[lo : lo + step, :] = mm.T
        y = y + nn(mm, wd[lo : lo + step, :])
        dgel = half + a * (jnp.exp(-0.5 * a * a) * (1.0 / math.sqrt(2.0 * math.pi)))
        ga = (gm * b * dgel).astype(BF)
        gb = (gm * gel).astype(BF)
        gu_o[:, lo : lo + step] = ga
        gu_o[:, ff + lo : ff + lo + step] = gb
        gn2 = gn2 + nt(ga, wi[:, lo : lo + step]) + nt(gb, wi[:, ff + lo : ff + lo + step])
    out[...] = y.astype(BF)

    t = gn2 * g
    gh2 = gyb.astype(F32) + r2 * (t - jnp.mean(t, axis=-1, keepdims=True) - nh * jnp.mean(t * nh, axis=-1, keepdims=True))
    gb16 = gh2.astype(BF)
    gh2b_o[...] = gb16
    go = nt(gb16, wo[...]).astype(BF)
    go_o[...] = go
    prod = go.astype(F32) * o[...].astype(F32)
    hi = prod.astype(BF)
    lo_part = (prod - hi.astype(F32)).astype(BF)
    sums = nt(ind[...], hi) + nt(ind[...], lo_part)
    for p in range(dlt.shape[0]):
        dlt[p] = sums[2 * p : 2 * p + 2, :]


def mid_call(sz, scal, pieces, x, o, gy, g2, ff):
    tok, width = x.shape
    heads = jnp.arange(16, dtype=jnp.int32)
    ind = (heads[:, None] == (jnp.arange(width, dtype=jnp.int32) // HEAD_DIM)[None, :]).astype(BF)
    row = lambda i, s: (i, 0)
    fix = lambda i, s: (0, 0)
    rs = lambda n: pl.BlockSpec((RB, n), row)
    cs = lambda n: pl.BlockSpec((n, RB), lambda i, s: (0, i))
    fs = lambda a: pl.BlockSpec(a.shape, fix)
    sh = jax.ShapeDtypeStruct
    n = len(pieces)
    return pl.pallas_call(
        functools.partial(mid_kernel, n, sz.places),
        grid_spec=pltpu.PrefetchScalarGridSpec(
            num_scalar_prefetch=1,
            grid=(tok // RB,),
            in_specs=[*[pl.BlockSpec(memory_space=pl.ANY)] * n, rs(width), rs(width), rs(width), fs(g2), fs(ind)],
            out_specs=[rs(width), cs(ff), rs(2 * ff), cs(width), rs(width), rs(width),
                       pl.BlockSpec((width // LANES, 2, RB), lambda i, s: (0, 0, i))],
            scratch_shapes=[pltpu.VMEM((width, width), BF), pltpu.VMEM((width, 2 * ff), BF), pltpu.VMEM((ff, width), BF),
                            pltpu.SemaphoreType.DMA((n, 2 * ff // width + 2))],
        ),
        out_shape=[sh((tok, width), BF), sh((ff, tok), BF), sh((tok, 2 * ff), BF), sh((width, tok), BF),
                   sh((tok, width), BF), sh((tok, width), BF),
                   sh((width // LANES, 2, tok), F32)],
        compiler_params=params(60, dimension_semantics=("arbitrary",)),
        cost_estimate=pl.CostEstimate(flops=13_000_000_000 * 2, bytes_accessed=30_000_000, transcendentals=0),
        name="middle",
    )(scal, *pieces, x, o, gy, g2, ind)


def put_halves(core, keep, send, rows0, values, n_group):
    rows = values.shape[0] // n_group
    half = half_of(rows)

    def store(first, second):
        for g in range(n_group):
            lo, hi = rows * g, rows * (g + 1)
            first[g, pl.ds(rows0, half), :] = values[lo : lo + half, :]
            second[g, pl.ds(rows0, half), :] = values[hi - half : hi, :]

    @pl.when(core == 0)
    def _():
        store(keep, send)

    @pl.when(core != 0)
    def _():
        store(send, keep)


def put_halves(core, keep, send, rows0, values, n_group):
    rows = values.shape[0] // n_group
    half = half_of(rows)

    def store(first, second):
        for g in range(n_group):
            lo, hi = rows * g, rows * (g + 1)
            first[g, pl.ds(rows0, half), :] = values[lo : lo + half, :]
            second[g, pl.ds(rows0, half), :] = values[hi - half : hi, :]

    @pl.when(core == 0)
    def _():
        store(keep, send)

    @pl.when(core != 0)
    def _():
        store(send, keep)


def in_grad_kernel(n_group, at, scal, n2t, gu, keep, send):
    half = half_of(n2t.shape[0] // n_group)
    row0 = pl.multiple_of(pl.program_id(0) * half, 16)
    put_halves(scal[at] % 2, keep, send, row0, nn(n2t[...], gu[...]).astype(BF), n_group)


def in_grad_call(sz, scal, n2t, gu, n_group):
    width, tok = n2t.shape
    n_cols = gu.shape[1] // width
    rows = n_cols * half_of(width // n_group)
    out = jax.ShapeDtypeStruct((n_group, rows, width), BF)
    return pl.pallas_call(
        functools.partial(in_grad_kernel, n_group, sz.places),
        grid_spec=pltpu.PrefetchScalarGridSpec(
            num_scalar_prefetch=1,
            grid=(n_cols,),
            in_specs=[pl.BlockSpec((width, tok), lambda j, s: (0, 0)), pl.BlockSpec((tok, width), lambda j, s: (0, j))],
            out_specs=[pl.BlockSpec((n_group, rows, width), lambda j, s: (0, 0, 0))] * 2,
        ),
        out_shape=[out, out],
        compiler_params=params(60, dimension_semantics=("arbitrary",)),
        cost_estimate=pl.CostEstimate(flops=8_000_000_000, bytes_accessed=10_000_000, transcendentals=0),
        name="in_weight_gradient",
    )(scal, n2t, gu)


def down_out_kernel(n_group, at, scal, mt, gy, ot_h, gh_h, keep, send, ot, gh, sem):
    copies = [pltpu.make_async_copy(ot_h, ot, sem.at[0]), pltpu.make_async_copy(gh_h, gh, sem.at[1])]
    for c in copies:
        c.start()
    put_halves(scal[at] % 2, keep, send, 0, nn(mt[...], gy[...]).astype(BF), n_group)
    for c in copies:
        c.wait()
    put_halves(scal[at] % 2, keep, send, half_of(mt.shape[0] // n_group), nn(ot[...], gh[...]).astype(BF), n_group)


def down_out_call(sz, scal, mt, gy, ot, gh, n_group):
    width, tok = ot.shape
    ff = mt.shape[0]
    rows = half_of(width // n_group) + half_of(ff // n_group)
    out = jax.ShapeDtypeStruct((n_group, rows, width), BF)
    anyspec = pl.BlockSpec(memory_space=pl.ANY)
    fix = lambda j, s: (0, 0)
    return pl.pallas_call(
        functools.partial(down_out_kernel, n_group, sz.places),
        grid_spec=pltpu.PrefetchScalarGridSpec(
            num_scalar_prefetch=1,
            grid=(1,),
            in_specs=[pl.BlockSpec((ff, tok), fix), pl.BlockSpec((tok, width), fix), anyspec, anyspec],
            out_specs=[pl.BlockSpec((n_group, rows, width), lambda j, s: (0, 0, 0))] * 2,
            scratch_shapes=[pltpu.VMEM((width, tok), BF), pltpu.VMEM((tok, width), BF), pltpu.SemaphoreType.DMA((2,))],
        ),
        out_shape=[out, out],
        compiler_params=params(60, dimension_semantics=("arbitrary",)),
        cost_estimate=pl.CostEstimate(flops=7_000_000_000, bytes_accessed=10_000_000, transcendentals=0),
        name="down_out_weight_gradients",
    )(scal, mt, gy, ot, gh)


def bwd_kernel(sz, pg, n_group, scal, q, k, v, kt, qf, kf, gl, gc, gr, lse_c, dlt_c, lse_l, dlt_l, lse_r, dlt_r,
               cos, sin, n1t, grad, keep, send, q2, g2, gka, gva, gqa, st, s_a, p_a, s_b, p_b):
    n_qb, tok = sz.n_qb, sz.tok
    q_lo, q_hi = scal[sz.q_lo], scal[sz.q_hi]
    for row, parts in ((0, (lse_l, lse_c, lse_r)), (1, (dlt_l, dlt_c, dlt_r))):
        for p in range(pg):
            at = 0
            for part in parts:
                for b in range(part.shape[2] // QB):
                    for h in range(2):
                        st[at, p, row : row + 1, QB * h : QB * h + QB] = part[p, h : h + 1, QB * b : QB * b + QB]
                    at += 1

    def prep(src, first, count):
        def one(i, _):
            r0 = pl.multiple_of(i * QB, QB)
            fq = qf[pl.ds(r0, QB), :]
            f2 = jnp.concatenate([fq, fq], axis=0)
            for p in range(pg):
                q2[i, p] = jnp.concatenate([split_heads(q[pl.ds(r0, QB), lanes_of(p)]), f2], axis=1)
                g2[i, p] = split_heads(src[pl.ds(pl.multiple_of((i - first) * QB, QB), QB), lanes_of(p)])
                gqa[i, p] = jnp.zeros((LANES, 2 * QB), F32)
                gka[p, pl.ds(r0, QB), :] = jnp.zeros((QB, LANES), F32)
                gva[p, pl.ds(r0, QB), :] = jnp.zeros((QB, LANES), F32)
            return 0

        lax.fori_loop(jnp.maximum(first, q_lo), jnp.minimum(first + count, q_hi), one, 0)

    prep(gl, 0, sz.own_lo)
    prep(gc, sz.own_lo, sz.own_qb)
    prep(gr, sz.own_hi, sz.own_lo)

    def tile(i):
        return jnp.minimum(scal[sz.bwd_q + i], q_hi - 1), pl.multiple_of(scal[sz.bwd_k + i] * QB, QB)

    def score_tile(i, s_buf, p_buf):
        qi, k0 = tile(i)
        fk = kf[pl.ds(k0, KB), :]
        for p in range(pg):
            s_buf[p] = nt(jnp.concatenate([k[pl.ds(k0, KB), lanes_of(p)], fk], axis=1), q2[qi, p])
            p_buf[p] = nt(v[pl.ds(k0, KB), lanes_of(p)], g2[qi, p])

    def grad_tile(i, s_buf, p_buf):
        qi, k0 = tile(i)
        dead = jnp.where(i < scal[sz.bwd_n], 0.0, 1e38).astype(F32)
        for p in range(pg):
            pr = jnp.exp2(s_buf[p] - (st[qi, p, 0:1, :] + dead))
            ds = (pr * (p_buf[p] - st[qi, p, 1:2, :])).astype(BF)
            gva[p, pl.ds(k0, KB), :] += nn(pr.astype(BF), g2[qi, p])
            gka[p, pl.ds(k0, KB), :] += nn(ds, q2[qi, p, :, :LANES])
            gqa[qi, p] += nn(kt[lanes_of(p), pl.ds(k0, KB)], ds)

    score_tile(0, s_a, p_a)

    def body(j, _):
        score_tile(2 * j + 1, s_b, p_b)
        grad_tile(2 * j, s_a, p_a)
        score_tile(2 * j + 2, s_a, p_a)
        grad_tile(2 * j + 1, s_b, p_b)
        return 0

    lax.fori_loop(0, (scal[sz.bwd_n] + 1) // 2, body, 0)

    sc = HEAD_DIM ** -0.5
    wide = LANES * pg

    def finish(i, _):
        o0 = pl.multiple_of(i * QB, QB)
        r0 = pl.multiple_of(HALO + i * QB, QB)
        co, si = cos[pl.ds(r0, QB), :], sin[pl.ds(r0, QB), :]
        for p in range(pg):
            a = gqa[sz.own_lo + i, p]
            gt = jnp.concatenate([a[:HEAD_DIM, :QB], a[HEAD_DIM:, QB:]], axis=0).T * sc
            grad[pl.ds(o0, QB), LANES * p : LANES * p + LANES] = (gt * co - partner(gt) * si).astype(BF)
            b = gka[p, pl.ds(r0, QB), :] * LN2
            lo = wide + LANES * p
            grad[pl.ds(o0, QB), lo : lo + LANES] = (b * co - partner(b) * si).astype(BF)
            lo = 2 * wide + LANES * p
            grad[pl.ds(o0, QB), lo : lo + LANES] = gva[p, pl.ds(r0, QB), :].astype(BF)
        return 0

    lax.fori_loop(0, sz.own_qb, finish, 0)
    for part in range(3):
        cols = slice(wide * part, wide * part + wide)
        values = nn(n1t[...], grad[:, cols]).astype(BF)
        put_halves(scal[sz.places] % 2, keep.at[:, :, cols], send.at[:, :, cols], 0, values, n_group)


def bwd_call(sz, scal, qkv, kt, qf, kf, gl, gc, gr, lse, dlt, st_l, st_r, cos, sin, n1t, pg, at, n_group):
    ext, tok, width, n_qb = sz.ext, sz.tok, sz.width, sz.n_qb
    pairs = width // LANES
    steps = pairs // pg
    wide = LANES * pg
    half = half_of(width // n_group)
    spec = lambda shape, *idx: pl.BlockSpec(shape, lambda i, s: idx, pipeline_mode=pl.Buffered(1))
    sh = jax.ShapeDtypeStruct
    side = [spec((pg, 2, HALO), at, 0, 0), spec((pg, 2, HALO), steps + at, 0, 0)]
    return pl.pallas_call(
        functools.partial(bwd_kernel, sz, pg, n_group),
        grid_spec=pltpu.PrefetchScalarGridSpec(
            num_scalar_prefetch=1,
            grid=(1,),
            in_specs=[
                spec((ext, wide), 0, at),
                spec((ext, wide), 0, steps + at),
                spec((ext, wide), 0, 2 * steps + at),
                spec((wide, ext), at, 0),
                spec((ext, LANES), 0, 0),
                spec((ext, LANES), 0, 0),
                spec((HALO, wide), 0, at),
                spec((tok, wide), 0, at),
                spec((HALO, wide), 0, at),
                spec((pg, 2, tok), at, 0, 0),
                spec((pg, 2, tok), at, 0, 0),
                *side,
                *side,
                spec((ext, LANES), 0, 0),
                spec((ext, LANES), 0, 0),
                spec((width, tok), 0, 0),
            ],
            out_specs=[spec((tok, 3 * wide), 0, 0), spec((n_group, half, 3 * wide), 0, 0, 0), spec((n_group, half, 3 * wide), 0, 0, 0)],
            scratch_shapes=[
                pltpu.VMEM((n_qb, pg, 2 * QB, 2 * LANES), BF),
                pltpu.VMEM((n_qb, pg, 2 * QB, LANES), BF),
                pltpu.VMEM((pg, ext, LANES), F32),
                pltpu.VMEM((pg, ext, LANES), F32),
                pltpu.VMEM((n_qb, pg, LANES, 2 * QB), F32),
                pltpu.VMEM((n_qb, pg, 8, 2 * QB), F32),
                *[pltpu.VMEM((pg, KB, 2 * QB), F32)] * 4,
            ],
        ),
        out_shape=[sh((tok, 3 * wide), BF), sh((n_group, half, 3 * wide), BF), sh((n_group, half, 3 * wide), BF)],
        compiler_params=params(60, dimension_semantics=("arbitrary",)),
        cost_estimate=pl.CostEstimate(flops=35_000_000_000, bytes_accessed=20_000_000, transcendentals=0),
        name="attn_backward",
    )(scal, qkv, qkv, qkv, kt, qf, kf, gl, gc, gr, lse, dlt, st_l, st_l, st_r, st_r, cos, sin, n1t)


def gx_kernel(n_pieces, n_grads, at, scal, *refs):
    pieces, grads = refs[:n_pieces], refs[n_pieces : n_pieces + n_grads]
    x, gh2, g1, out, w, sem = refs[n_pieces + n_grads :]

    @pl.when(pl.program_id(0) == 0)
    def _():
        copies = fetch_qkv(lambda t: scal[at + t], pieces, w, sem)
        for c in copies:
            c.start()
        for c in copies:
            c.wait()

    width = x.shape[1]
    gn = None
    wide = grads[0].shape[1] // 3
    for part in range(3):
        lhs = jnp.concatenate([grad[:, wide * part : wide * part + wide] for grad in grads], axis=1)
        term = nt(lhs, w[:, width * part : width * part + width])
        gn = term if gn is None else gn + term
    xf = x[...].astype(F32)
    mean = jnp.mean(xf, axis=-1, keepdims=True)
    cen = xf - mean
    r1 = lax.rsqrt(jnp.mean(cen * cen, axis=-1, keepdims=True) + EPS)
    nh = cen * r1

    t = gn * g1[...]
    gx = gh2[...].astype(F32) + r1 * (t - jnp.mean(t, axis=-1, keepdims=True) - nh * jnp.mean(t * nh, axis=-1, keepdims=True))
    out[...] = gx.astype(BF)


def gx_call(sz, scal, pieces, grads, x, gh2, g1):
    tok, width = x.shape
    row = lambda i, s: (i, 0)
    fix = lambda i, s: (0, 0)
    rs = pl.BlockSpec((RB, width), row)
    n = len(pieces)
    return pl.pallas_call(
        functools.partial(gx_kernel, n, len(grads), sz.places),
        grid_spec=pltpu.PrefetchScalarGridSpec(
            num_scalar_prefetch=1,
            grid=(tok // RB,),
            in_specs=[*[pl.BlockSpec(memory_space=pl.ANY)] * n,
                      *[pl.BlockSpec((RB, g.shape[1]), row) for g in grads],
                      rs, rs, pl.BlockSpec(g1.shape, fix)],
            out_specs=rs,
            scratch_shapes=[pltpu.VMEM((width, 3 * width), BF), pltpu.SemaphoreType.DMA((n,))],
        ),
        out_shape=jax.ShapeDtypeStruct((tok, width), BF),
        compiler_params=params(60, dimension_semantics=("arbitrary",)),
        cost_estimate=pl.CostEstimate(flops=4_000_000_000, bytes_accessed=15_000_000, transcendentals=0),
        name="input_gradient",
    )(scal, *pieces, *grads, x, gh2, g1)


class Net:
    def __init__(self, n_replica, n_group):
        self.n_replica, self.n_group, self.n_z = n_replica, n_group, n_replica // 2
        self.replica, self.group = lax.axis_index("replica"), lax.axis_index("group")
        self.core = self.replica & 1

    def shift(self, a, step):
        pairs = [(i, i + step) for i in range(self.n_replica) if 0 <= i + step < self.n_replica]
        return lax.ppermute(a, "replica", pairs)

    def core_swap(self, a):
        return lax.ppermute(a, "replica", [(i, i ^ 1) for i in range(self.n_replica)])

    def across(self, a, k):
        return lax.ppermute(a, "group", [(i, i ^ k) for i in range(self.n_group)])

    def across_swap(self, a, k):
        n = self.n_group
        pairs = [(r * n + g, (r ^ 1) * n + (g ^ k)) for r in range(self.n_replica) for g in range(n)]
        return lax.ppermute(a, ("replica", "group"), pairs)

    def gather_near(self, mine, other):
        got = {(0, 0): mine, (0, 1): other}
        for k in (1, 2) if self.n_group == 4 else range(1, self.n_group):
            got[k, 0] = self.across(mine, k)
        return got

    def gather_far(self, got):
        got = dict(got)
        if self.n_group == 4:
            got[3, 0] = self.across(got[2, 0], 1)
            got[3, 1] = self.across_swap(got[1, 0], 2)
        for k in range(1, self.n_group):
            if (k, 1) not in got:
                got[k, 1] = self.core_swap(got[k, 0])
        return [got[key] for key in sorted(got)]

    def parts(self, pairs):
        def part(k):
            at = lambda a: lax.dynamic_index_in_dim(a, self.group ^ k, 0, keepdims=False).astype(F32)
            return jnp.concatenate([at(keep) + at(got) for got, keep in pairs], axis=0)

        return [part(0)] + [part(k).astype(BF) for k in range(1, self.n_group)]

    def group_sum(self, parts):
        s = parts[0]
        for k in range(1, self.n_group):
            s = s + self.across(parts[k], k).astype(F32)
        return s

    def z_steps(self):
        z = self.replica // 2
        if self.n_z == 4:
            def first(s):
                a = lax.ppermute(s.astype(BF), "replica", [(0, 2), (1, 3), (6, 4), (7, 5)])
                return (s + a.astype(F32)).astype(BF)

            def second(s):
                b = lax.ppermute(s, "replica", [(2, 4), (3, 5), (4, 2), (5, 3)])
                return (s.astype(F32) + b.astype(F32)).astype(BF)

            def third(t):
                c = lax.ppermute(t, "replica", [(2, 0), (3, 1), (4, 6), (5, 7)])
                return jnp.where((z == 0) | (z == 3), c, t)

            return [first, second, third]

        def fold(k):
            def step(t):
                t = t.astype(BF)
                b = lax.ppermute(t, "replica", [(i, i ^ k) for i in range(self.n_replica)])
                return (t.astype(F32) + b.astype(F32)).astype(BF)
            return step

        return [fold(2 << i) for i in range(self.n_z.bit_length() - 1)]


def on_device(tokens, cotangent, lengths, dealing, offsets, attn_gain, qkv_weight, out_weight,
              mlp_gain, in_weight, down_weight, *, n_replica, n_group):
    net = Net(n_replica, n_group)
    x, gy = tokens[0], cotangent[0]
    tok, width = x.shape
    ff = in_weight.shape[1] // 2
    sz = Sizes(tok, width)
    pairs = width // LANES
    pg = 3
    tie = lax.optimization_barrier

    def half_rows(a, h):
        n = half_of(a.shape[0])
        return lax.dynamic_slice_in_dim(a, (net.core ^ h) * (a.shape[0] - n), n, 0).astype(BF)

    def pack(h):
        wi = half_rows(in_weight, h)
        cols = [wi[:, width * j : width * j + width] for j in range(2 * ff // width)]
        return jnp.concatenate([half_rows(out_weight, h), *cols, half_rows(down_weight, h)], axis=0)

    near = net.gather_near(half_rows(qkv_weight, 0), half_rows(qkv_weight, 1))
    own_gain = jnp.stack([attn_gain, mlp_gain]).astype(BF)
    by_offset = [own_gain] + [net.across(own_gain, k) for k in range(1, n_group)]
    packs = pack(0), pack(1)
    where = jnp.stack([net.replica, net.group]).astype(jnp.int32)
    near, by_offset, packs, where = tie((near, by_offset, packs, where))
    scal, qf, kf, cos, sin = plan_call(sz, n_replica, n_group, where, lengths)

    x_l = net.shift(x[tok - HALO :], 1)
    x_r = net.shift(x[:HALO], -1)
    qkv_pieces = net.gather_far(near)
    by_offset = jnp.stack(by_offset)
    hit = (jnp.arange(n_group)[:, None] ^ net.group) == jnp.arange(n_group)[None, :]
    gains = jnp.sum(jnp.where(hit[:, :, None, None], by_offset[None].astype(F32), 0.0), axis=1)
    gains = gains.transpose(1, 0, 2).reshape(2, width)
    g1, g2 = gains[0:1], gains[1:2]
    packs, qkv_pieces, x_l, x_r, gains = tie((packs, qkv_pieces, x_l, x_r, gains))

    near = net.gather_near(*packs)
    qkv, kt, vt, n1t = qkv_call(sz, scal, x_l, x, x_r, qkv_pieces, g1, cos, sin)
    near, vt = tie((near, vt))
    mlp_pieces = net.gather_far(near)
    o, ot, lse = fwd_call(sz, scal, qkv, vt, qf, kf, pg)
    out, mt, gu, n2t, gh2b, go, dlt = mid_call(sz, scal, mlp_pieces, x, o, gy, g2, ff)

    go_l = net.shift(go[tok - HALO :], 1)
    go_r = net.shift(go[:HALO], -1)
    stats = jnp.concatenate([lse, dlt], axis=0)
    st_l = net.shift(stats[:, :, tok - HALO :], 1)
    st_r = net.shift(stats[:, :, :HALO], -1)

    keep_i, send_i = in_grad_call(sz, scal, n2t, gu, n_group)
    keep_d, send_d = down_out_call(sz, scal, mt, gy, ot, gh2b, n_group)
    mlp_parts = net.parts([(net.core_swap(send_i), keep_i), (net.core_swap(send_d), keep_d)])

    def attn_grad(at, dep):
        return bwd_call(sz, dep, qkv, kt, qf, kf, go_l, go, go_r, lse, dlt, st_l, st_r, cos, sin, n1t, pg, at, n_group)

    scal, mlp_parts = tie((scal, mlp_parts))
    grad0, keep0, send0 = attn_grad(0, scal)
    mlp_sum = net.group_sum(mlp_parts).astype(BF)
    parts0 = net.parts([(net.core_swap(send0), keep0)])
    scal, mlp_sum, parts0 = tie((scal, mlp_sum, parts0))
    z = net.z_steps()
    last = len(z) - 1
    mlp_sum = z[0](mlp_sum)
    grad1, keep1, send1 = attn_grad(1, scal)
    sum0 = net.group_sum(parts0)
    sum0, mlp_sum, scal, send1 = tie((sum0, mlp_sum, scal, send1))

    got1 = net.core_swap(send1)
    mlp_sum = z[1](mlp_sum)
    sum0 = z[0](sum0)
    got1, sum0 = tie((got1, sum0))
    gx = gx_call(sz, scal, qkv_pieces, [grad0, grad1], x, gh2b, g1)
    sum1 = net.group_sum(net.parts([(got1, keep1)]))
    sum0 = z[1](sum0)
    for i in range(2, last + 1):
        sum0, sum1, mlp_sum = tie((sum0, sum1, mlp_sum))
        sum1 = z[i - 2](sum1)
        sum0 = z[i](sum0)
        mlp_sum = z[i](mlp_sum)
    sum0, sum1 = tie((sum0, sum1))
    sum1 = z[last - 1](sum1)
    sib0 = net.core_swap(sum0)
    sib0, sum1, mlp_sum = tie((sib0, sum1, mlp_sum))
    sum1 = z[last](sum1)
    sib_mlp = net.core_swap(mlp_sum)
    sib_mlp, sum1 = tie((sib_mlp, sum1))
    sib1 = net.core_swap(sum1)

    def both(t, sib):
        first = net.core == 0
        return jnp.where(first, t, sib).astype(F32), jnp.where(first, sib, t).astype(F32)

    def rows_of(p, q, shard):
        return jnp.concatenate([p[: shard - p.shape[0]], q], axis=0)

    shard, shard_d = width // n_group, ff // n_group
    half, half_d = half_of(shard), half_of(shard_d)
    a, b = both(sum1, sib1)
    wide = LANES * pg
    qkv_half = lambda parts: jnp.concatenate([p[:half, wide * c : wide * c + wide] for c in range(3) for p in parts], axis=1)
    c, d = both(sum0, sib0)
    d_qkv = rows_of(qkv_half([c, a]), qkv_half([d, b]), shard)
    a, b = both(mlp_sum, sib_mlp)
    n_cols = 2 * ff // width
    wide_in = lambda p: jnp.concatenate([p[half * j : half * j + half] for j in range(n_cols)], axis=1)
    d_in = rows_of(wide_in(a), wide_in(b), shard)
    lo, hi = half * n_cols, half * n_cols + half_d
    d_down = rows_of(a[lo:hi], b[lo:hi], shard_d)
    d_out = rows_of(a[hi:], b[hi:], shard)
    low = lambda v: v.astype(BF).astype(F32)
    d_g1 = jnp.sum(low(qkv_weight) * d_qkv, axis=1) / low(attn_gain)
    d_g2 = jnp.sum(low(in_weight) * d_in, axis=1) / low(mlp_gain)
    return (out[None], gx[None], d_g1, d_qkv, d_out, d_g2, d_in, d_down)


def solution(mesh):
    body = functools.partial(on_device, n_replica=mesh.shape["replica"], n_group=mesh.shape["group"])
    return jax.shard_map(
        body,
        mesh=mesh,
        in_specs=(
            P("group", "replica", None),
            P("group", "replica", None),
            P("group", None),
            P("group", None),
            P("group", None, None),
            P("group"),
            P("group", None),
            P("group", None),
            P("group"),
            P("group", None),
            P("group", None),
        ),
        out_specs=(
            P("group", "replica", None),
            P("group", "replica", None),
            P("group"),
            P("group", None),
            P("group", None),
            P("group"),
            P("group", None),
            P("group", None),
        ),
        check_vma=False,
    )
```

time: 632 us -> 367 us (0.58)
  waiting for transfers between devices: 325 us -> 46.6 us
  starting transfers between devices: 15 us -> 93.1 us
  blocking collectives: 25.8 us -> 0 us
  matrix products: 23 us -> 0 us
  between operations: 17.2 us -> 1.61 us
  Pallas kernels: 175 us -> 189 us
  local copies, waits for them, and re-layouts: 27.4 us -> 17.1 us
    reduce_scatter x3 -> x0, waiting for transfers between devices: 115 us -> none  [reduce(): s = lax.psum_scatter(a.astype(BF), 'group', scatter_dimension=0, tiled=True)]
    unnamed x12 -> x0, waiting for transfers between devices: 86.6 us -> none
    ppermute x6 -> x46, starting transfers between devices: 14.3 us -> 93.1 us  [the longest x3 31.4 us: first(): a = lax.ppermute(s.astype(BF), 'replica', [(0, 2), (1, 3), (6, 4), (7, 5)])]
    all_gather x4 -> x0, waiting for transfers between devices: 65 us -> none  [on_device(): gather = lambda a: lax.all_gather(a.astype(BF), 'group', axis=0, tiled=True)]
    psum x1 -> x0, waiting for transfers between devices: 57.4 us -> none  [reduce(): return lax.psum(s, 'replica').astype(F32)]
    ppermute x6 -> x46, waiting for transfers between devices: 0.02 us -> 46.6 us  [the longest x3 29.2 us: third(): c = lax.ppermute(t, 'replica', [(2, 0), (3, 1), (4, 6), (5, 7)])]
    dot_general x6 -> x0, matrix products: 23 us -> none  [tn(): lax.dot_general(a, b, (((0,), (0,)), ((), ())), preferred_element_type=F32)]
    psum x1 -> x0, blocking collectives: 16.3 us -> none  [reduce(): return lax.psum(s, 'replica').astype(F32)]
  transfers between devices with their start and end apart: 16 -> 46, of which waited for: 8 -> 9; matrix products, arithmetic and copies ran while one was open for 7% -> 6% of each run, Pallas kernels for 12% -> 41%
where the time goes in v2:
time: 367 us; the launch traced here: 364 us
  Pallas kernels  189 us (51%)
  starting transfers between devices  93.1 us (25%)
  waiting for transfers between devices  46.6 us (13%)
  local copies, waits for them, and re-layouts  17.1 us (5%)
  other arithmetic  16.4 us (4%)
    pallas_call x2, Pallas kernels, bwd_call(): pl.pallas_call(functools.partial(bwd_kernel, sz, pg, n_group), grid_spec=...  72.2 us
    ppermute x3, starting transfers between devices, first(): a = lax.ppermute(s.astype(BF), 'replica', [(0, 2), (1, 3), (6, 4), (7, 5)])  31.4 us
    ppermute x3, waiting for transfers between devices, third(): c = lax.ppermute(t, 'replica', [(2, 0), (3, 1), (4, 6), (5, 7)])  29.2 us
    pallas_call x1, Pallas kernels, mid_call(): pl.pallas_call(functools.partial(mid_kernel, n, sz.places), grid_spec=plt...  29.1 us
    ppermute x18, starting transfers between devices, across(): return lax.ppermute(a, 'group', [(i, i ^ k) for i in range(self.n_group)])  28.4 us
    pallas_call x1, Pallas kernels, fwd_call(): pl.pallas_call(functools.partial(fwd_kernel, sz, pg), grid_spec=pltpu.Pre...  26.2 us
    pallas_call x1, Pallas kernels, qkv_call(): pl.pallas_call(functools.partial(qkv_kernel, sz, len(pieces)), grid_spec=...  20.5 us
    ppermute x6, starting transfers between devices, shift(): return lax.ppermute(a, 'replica', pairs)  13.1 us
  transfers between devices with their start and end apart: 46, of which 9 were waited for; matrix products, arithmetic and copies ran while one was open for 6% of the time, Pallas kernels for 41%

profile of v2, /device:TPU:0, one launch (start us, length us, event | category | flops | bytes accessed | tf_op | source)
XLA Modules:
  0.0 363.7 jit_solution(17698952970757604169)
XLA Ops:
  0.7 2.4 dynamic-slice_convert_fusion.2
  3.1 2.9 collective-permute-start
  8.3 2.9 collective-permute-start.4
  11.3 1.9 fusion.17
  20.4 4.0 %collective-permute-start.9 = (bf16[768,768]{1,0:T(8,128)(2,1)}, bf16[768,768]{1,0:T(8,128)(2,1)}, u32[]{:S(2)}, u32[]{:S(2)}) collective-permute-start(bf16[768,768]{1,0:T(8,128)(2,1)} %get-tuple-element.214), channel_id=1, source_target_pairs={{0,4},{4,8},{8,12},{12,16},{16,20},{20,24},{24,28},{1,5},{5,9},{9,... | collective-permute-start | bytes 3538952 | tf_op jit(solution)/shard_map/ppermute | solution.py:831
  27.4 11.8 %plan.1 = (s32[382]{0:T(512)}, bf16[2816,128]{1,0:T(8,128)(2,1)}, bf16[2816,128]{1,0:T(8,128)(2,1)}, f32[2816,128]{1,0:T(8,128)}, f32[2816,128]{1,0:T(8,128)}) custom-call(s32[2]{0:T(128)} %pad_add_fusion.where, s32[1,16]{1,0:T(1,128)} %lengths.1), custom_call_target="tpu_custom_call" | custom-call | flops 10000000000 | bytes 5000000 | tf_op jit(solution)/shard_map/plan/pallas_call | solution.py:166
  43.7 20.5 %qkv.1 = (bf16[2816,2304]{1,0:T(8,128)(2,1)}, bf16[768,2816]{1,0:T(8,128)(2,1)}, bf16[768,2816]{1,0:T(8,128)(2,1)}, bf16[768,1024]{1,0:T(8,128)(2,1)}) custom-call(s32[382]{0:T(512)} %get-tuple-element.157.scal, bf16[768,768]{1,0:T(8,128)(2,1)} %collective-permute-done.9.xl, bf16[1024,768]{1,0:T(8,128)(2,1)} %bitcast.51, bf16[768,768]{1,0:T(8,128)(2,1)} %copy-done.21, ...), custom_call_target="tpu_custom_call" | custom-call | flops 14000000000 | bytes 30000000 | tf_op jit(solution)/shard_map/qkv/pallas_call | solution.py:245
  66.5 5.9 %collective-permute-start.16 = (bf16[528,768]{1,0:T(8,128)(2,1)S(1)}, bf16[528,768]{1,0:T(8,128)(2,1)}, u32[]{:S(2)}, u32[]{:S(2)}) collective-permute-start(bf16[528,768]{1,0:T(8,128)(2,1)S(1)} %collective-permute-done.11.refs_2_), channel_id=1, source_target_pairs={{0,6},{1,7},{2,4},{3,5},{4,2},{5,3},{6,0},{7,1},{8,14},{9,15},{10,... | collective-permute-start | bytes 2433032 | tf_op jit(solution)/shard_map/ppermute | solution.py:842
  72.4 26.2 %attn_forward.1 = (bf16[1024,768]{1,0:T(8,128)(2,1)}, bf16[768,1024]{1,0:T(8,128)(2,1)}, f32[6,2,1024]{2,1,0:T(2,128)}) custom-call(s32[382]{0:T(512)} %get-tuple-element.157.scal, bf16[2816,2304]{1,0:T(8,128)(2,1)} %get-tuple-element.123.q.k.v, bf16[2816,2304]{1,0:T(8,128)(2,1)} %get-tuple-element.123.q.k.v, bf16[768,2816]{1,0:T(8,128)(2,1)} %get-tuple-element.124.vt, ...), custom_call_target="tpu_custom_call" | custom-call | flops 30000001024 | bytes 15000000 | tf_op jit(solution)/shard_map/attn_forward/pallas_call | solution.py:391
  99.8 29.1 %middle.1 = (bf16[1024,768]{1,0:T(8,128)(2,1)}, bf16[1152,1024]{1,0:T(8,128)(2,1)}, bf16[1024,2304]{1,0:T(8,128)(2,1)}, bf16[768,1024]{1,0:T(8,128)(2,1)}, bf16[...) custom-call(s32[382]{0:T(512)} %get-tuple-element.157.scal, ...), custom_call_target="tpu_custom_call" | custom-call | flops 25999998976 | bytes 30000000 | tf_op jit(solution)/shard_map/middle/pallas_call | solution.py:514
  129.0 8.9 %in_weight_gradient.1 = (bf16[4,288,768]{2,1,0:T(8,128)(2,1)}, bf16[4,288,768]{2,1,0:T(8,128)(2,1)}) custom-call(s32[382]{0:T(512)} %get-tuple-element.157.scal, bf16[768,1024]{1,0:T(8,128)(2,1)} %get-tuple-element.129.n2t, bf16[1024,2304]{1,0:T(8,128)(2,1)} %get-tuple-element.130.gu), custom_call_target="tpu_custom_call" | custom-call | flops 8000000000 | bytes 10000000 | tf_op jit(solution)/shard_map/in_weight_gradient/pallas_call | solution.py:583
  137.9 9.0 %down_out_weight_gradients.1 = (bf16[4,240,768]{2,1,0:T(8,128)(2,1)}, bf16[4,240,768]{2,1,0:T(8,128)(2,1)}) custom-call(s32[382]{0:T(512)} %get-tuple-element.157.scal, bf16[1152,1024]{1,0:T(8,128)(2,1)} %get-tuple-element.133.mt, bf16[1024,768]{1,0:T(8,128)(2,1)} %bitcast.60, bf16[768,1024]{1,0:T(8,128)(2,1)} %get-tuple-element.134.ot_h, ...), custom_call_target="tpu_custom_call" | custom-call | flops 7000000000 | bytes 10000000 | tf_op jit(solution)/shard_map/down_out_weight_gradients/pallas_call | solution.py:615
  147.7 2.2 collective-permute-start.22
  151.3 3.0 collective-permute-start.24
  155.6 1.8 fusion.7
  157.5 1.8 fusion.2
  163.2 3.1 collective-permute-start.20
  168.9 36.0 %attn_backward.2 = (bf16[1024,1152]{1,0:T(8,128)(2,1)}, bf16[4,96,1152]{2,1,0:T(8,128)(2,1)}, bf16[4,96,1152]{2,1,0:T(8,128)(2,1)}) custom-call(s32[382]{0:T(512)} %get-tuple-element.157.scal, bf16[2816,2304]{1,0:T(8,128)(2,1)} %get-tuple-element.123.q.k.v, bf16[2816,2304]{1,0:T(8,128)(2,1)} %get-tuple-element.123.q.k.v, ...), custom_call_target="tpu_custom_call" | custom-call | flops 35000000512 | bytes 20000000 | tf_op jit(solution)/shard_map/attn_backward/pallas_call | solution.py:728
  204.9 5.1 %collective-permute-start.26 = (bf16[4,96,1152]{2,1,0:T(8,128)(2,1)}, bf16[4,96,1152]{2,1,0:T(8,128)(2,1)S(1)}, u32[]{:S(2)}, u32[]{:S(2)}) collective-permute-start(bf16[4,96,1152]{2,1,0:T(8,128)(2,1)} %get-tuple-element.149), channel_id=1, source_target_pairs={{0,4},{4,0},{8,12},{12,8},{16,20},{20,16},{24,28},{28,24},{1,5},{5... | collective-permute-start | bytes 2654216 | tf_op jit(solution)/shard_map/ppermute | solution.py:834
  212.6 8.2 %collective-permute-start.30 = (bf16[528,768]{1,0:T(8,128)(2,1)S(1)}, bf16[528,768]{1,0:T(8,128)(2,1)S(1)}, u32[]{:S(2)}, u32[]{:S(2)}) collective-permute-start(bf16[528,768]{1,0:T(8,128)(2,1)S(1)} %add_convert_fusion.2), channel_id=1, source_target_pairs={{0,8},{4,12},{24,16},{28,20},{1,9},{5,13},{25,17},{29,21},{2,10},{... | collective-permute-start | bytes 2433032 | tf_op jit(solution)/shard_map/ppermute | solution.py:877
  220.8 4.3 %collective-permute-start.28 = (bf16[96,1152]{1,0:T(8,128)(2,1)S(1)}, bf16[96,1152]{1,0:T(8,128)(2,1)S(1)}, u32[]{:S(2)}, u32[]{:S(2)}) collective-permute-start(bf16[96,1152]{1,0:T(8,128)(2,1)S(1)} %get-tuple-element.152), channel_id=1, source_target_pairs={{0,2},{1,3},{2,0},{3,1},{4,6},{5,7},{6,4},{7,5},{8,10},{9,11},{10,... | collective-permute-start | bytes 663560 | tf_op jit(solution)/shard_map/ppermute | solution.py:837
  225.1 36.2 %attn_backward.3 = (bf16[1024,1152]{1,0:T(8,128)(2,1)}, bf16[4,96,1152]{2,1,0:T(8,128)(2,1)}, bf16[4,96,1152]{2,1,0:T(8,128)(2,1)}) custom-call(s32[382]{0:T(512)} %get-tuple-element.157.scal, bf16[2816,2304]{1,0:T(8,128)(2,1)} %get-tuple-element.123.q.k.v, bf16[2816,2304]{1,0:T(8,128)(2,1)} %get-tuple-element.123.q.k.v, ...), custom_call_target="tpu_custom_call" | custom-call | flops 35000000512 | bytes 20000000 | tf_op jit(solution)/shard_map/attn_backward/pallas_call | solution.py:728
  262.6 7.7 %collective-permute-start.32 = (bf16[96,1152]{1,0:T(8,128)(2,1)S(1)}, bf16[96,1152]{1,0:T(8,128)(2,1)S(1)}, u32[]{:S(2)}, u32[]{:S(2)}) collective-permute-start(bf16[96,1152]{1,0:T(8,128)(2,1)S(1)} %convert_element_type.377), channel_id=1, source_target_pairs={{0,8},{4,12},{24,16},{28,20},{1,9},{5,13},{25,17},{29,21},{2,10},{... | collective-permute-start | bytes 663560 | tf_op jit(solution)/shard_map/ppermute | solution.py:877
  270.4 3.3 collective-permute-done.32
  274.9 3.7 %collective-permute-start.34 = (bf16[96,1152]{1,0:T(8,128)(2,1)S(1)}, bf16[96,1152]{1,0:T(8,128)(2,1)S(1)}, u32[]{:S(2)}, u32[]{:S(2)}) collective-permute-start(bf16[96,1152]{1,0:T(8,128)(2,1)S(1)} %get-tuple-element.190), channel_id=1, source_target_pairs={{0,1},{1,0},{2,3},{3,2},{4,5},{5,4},{6,7},{7,6},{8,9},{9,8},{10,11... | collective-permute-start | bytes 663560 | tf_op jit(solution)/shard_map/ppermute | solution.py:837
  278.6 3.0 collective-permute-start.35
  281.7 3.0 collective-permute-done.34
  284.7 6.7 %collective-permute-done.35 = bf16[96,1152]{1,0:T(8,128)(2,1)S(1)} collective-permute-done((bf16[96,1152]{1,0:T(8,128)(2,1)S(1)}, bf16[96,1152]{1,0:T(8,128)(2,1)S(1)}, u32[]{:S(2)}, u32[]{:S(2)}) %collective-permute-start.35) | collective-permute-done | bytes 221216 | tf_op jit(solution)/shard_map/ppermute | solution.py:837
  291.5 15.5 %collective-permute-start.39 = (bf16[96,1152]{1,0:T(8,128)(2,1)S(1)}, bf16[96,1152]{1,0:T(8,128)(2,1)S(1)}, u32[]{:S(2)}, u32[]{:S(2)}) collective-permute-start(bf16[96,1152]{1,0:T(8,128)(2,1)S(1)} %convert_element_type.403), channel_id=1, source_target_pairs={{0,8},{4,12},{24,16},{28,20},{1,9},{5,13},{25,17},{29,21},{2,10},{... | collective-permute-start | bytes 663560 | tf_op jit(solution)/shard_map/ppermute | solution.py:877
  311.5 21.5 %collective-permute-done.38 = bf16[96,1152]{1,0:T(8,128)(2,1)S(1)} collective-permute-done((bf16[96,1152]{1,0:T(8,128)(2,1)S(1)}, bf16[96,1152]{1,0:T(8,128)(2,1)S(1)}, u32[]{:S(2)}, u32[]{:S(2)}) %collective-permute-start.38) | collective-permute-done | bytes 221216 | tf_op jit(solution)/shard_map/ppermute | solution.py:885
  333.7 11.1 %input_gradient.1 = bf16[1024,768]{1,0:T(8,128)(2,1)} custom-call(s32[382]{0:T(512)} %get-tuple-element.157.scal, bf16[96,2304]{1,0:T(8,128)(2,1)} %copy-done.9, bf16[96,2304]{1,0:T(8,128)(2,1)} %get-tuple-element.105.rest_1_.refs_1_, bf16[96,2304]{1,0:T(8,128)(2,1)} %collective-permute-done.rest_2_.refs_2_, ...), custom_call_target="tpu_custom_call" | custom-call | flops 4000000000 | bytes 15000000 | tf_op jit(solution)/shard_map/input_gradient/pallas_call | solution.py:805
  347.9 7.8 %collective-permute-done.44 = bf16[96,1152]{1,0:T(8,128)(2,1)S(1)} collective-permute-done((bf16[96,1152]{1,0:T(8,128)(2,1)S(1)}, bf16[96,1152]{1,0:T(8,128)(2,1)S(1)}, u32[]{:S(2)}, u32[]{:S(2)}) %collective-permute-start.44) | collective-permute-done | bytes 221216 | tf_op jit(solution)/shard_map/ppermute | solution.py:885
  (211 shorter events, 51.5 us)
Async XLA Ops:
  3.1 21.3 %collective-permute-start = (bf16[96,2304]{1,0:T(8,128)(2,1)S(1)}, bf16[96,2304]{1,0:T(8,128)(2,1)}, u32[]{:S(2)}, u32[]{:S(2)}) collective-permute-start(bf16[96,2304]{1,0:T(8,128)(2,1)S(1)} %get-tuple-element.104.rest_0_.refs_0_), channel_id=1, source_target_pairs={{0,1},{1,0},{2,3},{3,2},{4,5},{5,4},{6,7},{7,6},{8,9},{9,8},{10,11... | collective-permute-start | bytes 1327112 | tf_op jit(solution)/shard_map/ppermute | solution.py:837
  6.0 18.4 %collective-permute-start.1 = (bf16[96,2304]{1,0:T(8,128)(2,1)S(1)}, bf16[96,2304]{1,0:T(8,128)(2,1)}, u32[]{:S(2)}, u32[]{:S(2)}) collective-permute-start(bf16[96,2304]{1,0:T(8,128)(2,1)S(1)} %get-tuple-element.104.rest_0_.refs_0_), channel_id=1, source_target_pairs={{0,2},{1,3},{2,0},{3,1},{4,6},{5,7},{6,4},{7,5},{8,10},{9,11},{10,... | collective-permute-start | bytes 1327112 | tf_op jit(solution)/shard_map/ppermute | solution.py:837
  8.2 12.2 %collective-permute-start.3 = (bf16[2,192]{1,0:T(2,128)(2,1)S(1)}, bf16[2,192]{1,0:T(2,128)(2,1)S(1)}, u32[]{:S(2)}, u32[]{:S(2)}) collective-permute-start(bf16[2,192]{1,0:T(2,128)(2,1)S(1)} %pad_maximum_fusion.7), channel_id=1, source_target_pairs={{0,2},{1,3},{2,0},{3,1},{4,6},{5,7},{6,4},{7,5},{8,10},{9,11},{10,... | collective-permute-start | bytes 2312 | tf_op jit(solution)/shard_map/ppermute | solution.py:837
  8.3 16.2 %collective-permute-start.4 = (bf16[2,192]{1,0:T(2,128)(2,1)S(1)}, bf16[2,192]{1,0:T(2,128)(2,1)S(1)}, u32[]{:S(2)}, u32[]{:S(2)}) collective-permute-start(bf16[2,192]{1,0:T(2,128)(2,1)S(1)} %pad_maximum_fusion.7), channel_id=1, source_target_pairs={{0,3},{1,2},{2,1},{3,0},{4,7},{5,6},{6,5},{7,4},{8,11},{9,10},{10,... | collective-permute-start | bytes 2312 | tf_op jit(solution)/shard_map/ppermute | solution.py:837
  19.1 21.6 %collective-permute-start.10 = (bf16[768,768]{1,0:T(8,128)(2,1)}, bf16[768,768]{1,0:T(8,128)(2,1)S(1)}, u32[]{:S(2)}, u32[]{:S(2)}) collective-permute-start(bf16[768,768]{1,0:T(8,128)(2,1)} %get-tuple-element.213), channel_id=1, source_target_pairs={{4,0},{8,4},{12,8},{16,12},{20,16},{24,20},{28,24},{5,1},{9,5},{13... | collective-permute-start | bytes 3538952 | tf_op jit(solution)/shard_map/ppermute | solution.py:831
  20.4 20.3 %collective-permute-start.9 = (bf16[768,768]{1,0:T(8,128)(2,1)}, bf16[768,768]{1,0:T(8,128)(2,1)}, u32[]{:S(2)}, u32[]{:S(2)}) collective-permute-start(bf16[768,768]{1,0:T(8,128)(2,1)} %get-tuple-element.214), channel_id=1, source_target_pairs={{0,4},{4,8},{8,12},{12,16},{16,20},{20,24},{24,28},{1,5},{5,9},{9,... | collective-permute-start | bytes 3538952 | tf_op jit(solution)/shard_map/ppermute | solution.py:831
  25.4 15.3 %collective-permute-start.6 = (bf16[96,2304]{1,0:T(8,128)(2,1)}, bf16[96,2304]{1,0:T(8,128)(2,1)S(1)}, u32[]{:S(2)}, u32[]{:S(2)}) collective-permute-start(bf16[96,2304]{1,0:T(8,128)(2,1)} %collective-permute-done.1.rest_4_.refs_4_), channel_id=1, source_target_pairs={{0,4},{4,0},{8,12},{12,8},{16,20},{20,16},{24,28},{28,24},{1,5},{5... | collective-permute-start | bytes 1327112 | tf_op jit(solution)/shard_map/ppermute | solution.py:834
  25.7 15.0 %collective-permute-start.7 = (bf16[96,2304]{1,0:T(8,128)(2,1)}, bf16[96,2304]{1,0:T(8,128)(2,1)S(1)}, u32[]{:S(2)}, u32[]{:S(2)}) collective-permute-start(bf16[96,2304]{1,0:T(8,128)(2,1)} %collective-permute-done.1.rest_4_.refs_4_), channel_id=1, source_target_pairs={{0,1},{1,0},{2,3},{3,2},{4,5},{5,4},{6,7},{7,6},{8,9},{9,8},{10,11... | collective-permute-start | bytes 1327112 | tf_op jit(solution)/shard_map/ppermute | solution.py:837
  26.9 13.8 %collective-permute-start.8 = (bf16[96,2304]{1,0:T(8,128)(2,1)}, bf16[96,2304]{1,0:T(8,128)(2,1)}, u32[]{:S(2)}, u32[]{:S(2)}) collective-permute-start(bf16[96,2304]{1,0:T(8,128)(2,1)} %collective-permute-done.rest_2_.refs_2_), channel_id=1, source_target_pairs={{0,6},{1,7},{2,4},{3,5},{4,2},{5,3},{6,0},{7,1},{8,14},{9,15},{10,... | collective-permute-start | bytes 1327112 | tf_op jit(solution)/shard_map/ppermute | solution.py:842
  41.6 22.5 %collective-permute-start.11 = (bf16[528,768]{1,0:T(8,128)(2,1)S(1)}, bf16[528,768]{1,0:T(8,128)(2,1)S(1)}, u32[]{:S(2)}, u32[]{:S(2)}) collective-permute-start(bf16[528,768]{1,0:T(8,128)(2,1)S(1)} %copy-done.14), channel_id=1, source_target_pairs={{0,1},{1,0},{2,3},{3,2},{4,5},{5,4},{6,7},{7,6},{8,9},{9,8},{10,11... | collective-permute-start | bytes 2433032 | tf_op jit(solution)/shard_map/ppermute | solution.py:837
  42.0 22.2 %collective-permute-start.12 = (bf16[528,768]{1,0:T(8,128)(2,1)S(1)}, bf16[528,768]{1,0:T(8,128)(2,1)S(1)}, u32[]{:S(2)}, u32[]{:S(2)}) collective-permute-start(bf16[528,768]{1,0:T(8,128)(2,1)S(1)} %copy-done.14), channel_id=1, source_target_pairs={{0,2},{1,3},{2,0},{3,1},{4,6},{5,7},{6,4},{7,5},{8,10},{9,11},{10,... | collective-permute-start | bytes 2433032 | tf_op jit(solution)/shard_map/ppermute | solution.py:837
  64.2 34.5 %collective-permute-start.14 = (bf16[528,768]{1,0:T(8,128)(2,1)S(1)}, bf16[528,768]{1,0:T(8,128)(2,1)S(1)}, u32[]{:S(2)}, u32[]{:S(2)}) collective-permute-start(bf16[528,768]{1,0:T(8,128)(2,1)S(1)} %collective-permute-done.12.refs_4_), channel_id=1, source_target_pairs={{0,4},{4,0},{8,12},{12,8},{16,20},{20,16},{24,28},{28,24},{1,5},{5... | collective-permute-start | bytes 2433032 | tf_op jit(solution)/shard_map/ppermute | solution.py:834
  65.2 33.4 %collective-permute-start.15 = (bf16[528,768]{1,0:T(8,128)(2,1)S(1)}, bf16[528,768]{1,0:T(8,128)(2,1)S(1)}, u32[]{:S(2)}, u32[]{:S(2)}) collective-permute-start(bf16[528,768]{1,0:T(8,128)(2,1)S(1)} %collective-permute-done.12.refs_4_), channel_id=1, source_target_pairs={{0,1},{1,0},{2,3},{3,2},{4,5},{5,4},{6,7},{7,6},{8,9},{9,8},{10,11... | collective-permute-start | bytes 2433032 | tf_op jit(solution)/shard_map/ppermute | solution.py:837
  66.5 32.1 %collective-permute-start.13 = (bf16[528,768]{1,0:T(8,128)(2,1)S(1)}, bf16[528,768]{1,0:T(8,128)(2,1)}, u32[]{:S(2)}, u32[]{:S(2)}) collective-permute-start(bf16[528,768]{1,0:T(8,128)(2,1)S(1)} %collective-permute-done.11.refs_2_), channel_id=1, source_target_pairs={{0,4},{4,0},{8,12},{12,8},{16,20},{20,16},{24,28},{28,24},{1,5},{5... | collective-permute-start | bytes 2433032 | tf_op jit(solution)/shard_map/ppermute | solution.py:834
  66.5 32.2 %collective-permute-start.16 = (bf16[528,768]{1,0:T(8,128)(2,1)S(1)}, bf16[528,768]{1,0:T(8,128)(2,1)}, u32[]{:S(2)}, u32[]{:S(2)}) collective-permute-start(bf16[528,768]{1,0:T(8,128)(2,1)S(1)} %collective-permute-done.11.refs_2_), channel_id=1, source_target_pairs={{0,6},{1,7},{2,4},{3,5},{4,2},{5,3},{6,0},{7,1},{8,14},{9,15},{10,... | collective-permute-start | bytes 2433032 | tf_op jit(solution)/shard_map/ppermute | solution.py:842
  137.9 19.6 %collective-permute-start.17 = (bf16[4,288,768]{2,1,0:T(8,128)(2,1)}, bf16[4,288,768]{2,1,0:T(8,128)(2,1)}, u32[]{:S(2)}, u32[]{:S(2)}) collective-permute-start(bf16[4,288,768]{2,1,0:T(8,128)(2,1)} %get-tuple-element.132), channel_id=1, source_target_pairs={{0,4},{4,0},{8,12},{12,8},{16,20},{20,16},{24,28},{28,24},{1,5},{5... | collective-permute-start | bytes 5308424 | tf_op jit(solution)/shard_map/ppermute | solution.py:834
  147.7 19.2 %collective-permute-start.22 = (bf16[768,768]{1,0:T(8,128)(2,1)S(1)}, bf16[768,768]{1,0:T(8,128)(2,1)S(1)}, u32[]{:S(2)}, u32[]{:S(2)}) collective-permute-start(bf16[768,768]{1,0:T(8,128)(2,1)S(1)} %get-tuple-element.212), channel_id=1, source_target_pairs={{0,4},{4,8},{8,12},{12,16},{16,20},{20,24},{24,28},{1,5},{5,9},{9,... | collective-permute-start | bytes 3538952 | tf_op jit(solution)/shard_map/ppermute | solution.py:831
  149.9 17.0 %collective-permute-start.23 = (bf16[768,768]{1,0:T(8,128)(2,1)S(1)}, bf16[768,768]{1,0:T(8,128)(2,1)S(1)}, u32[]{:S(2)}, u32[]{:S(2)}) collective-permute-start(bf16[768,768]{1,0:T(8,128)(2,1)S(1)} %get-tuple-element.211), channel_id=1, source_target_pairs={{4,0},{8,4},{12,8},{16,12},{20,16},{24,20},{28,24},{5,1},{9,5},{13... | collective-permute-start | bytes 3538952 | tf_op jit(solution)/shard_map/ppermute | solution.py:831
  151.3 12.0 %collective-permute-start.24 = (f32[12,2,768]{2,1,0:T(2,128)S(1)}, f32[12,2,768]{2,1,0:T(2,128)S(1)}, u32[]{:S(2)}, u32[]{:S(2)}) collective-permute-start(f32[12,2,768]{2,1,0:T(2,128)S(1)} %get-tuple-element.224), channel_id=1, source_target_pairs={{0,4},{4,8},{8,12},{12,16},{16,20},{20,24},{24,28},{1,5},{5,9},{9,... | collective-permute-start | bytes 221192 | tf_op jit(solution)/shard_map/ppermute | solution.py:831
  154.3 12.0 %collective-permute-start.25 = (f32[12,2,768]{2,1,0:T(2,128)S(1)}, f32[12,2,768]{2,1,0:T(2,128)S(1)}, u32[]{:S(2)}, u32[]{:S(2)}) collective-permute-start(f32[12,2,768]{2,1,0:T(2,128)S(1)} %get-tuple-element.223), channel_id=1, source_target_pairs={{4,0},{8,4},{12,8},{16,12},{20,16},{24,20},{28,24},{5,1},{9,5},{13... | collective-permute-start | bytes 221192 | tf_op jit(solution)/shard_map/ppermute | solution.py:831
  161.5 48.6 %collective-permute-start.19 = (bf16[528,768]{1,0:T(8,128)(2,1)}, bf16[528,768]{1,0:T(8,128)(2,1)S(1)}, u32[]{:S(2)}, u32[]{:S(2)}) collective-permute-start(bf16[528,768]{1,0:T(8,128)(2,1)} %pad_maximum_fusion.3), channel_id=1, source_target_pairs={{0,1},{1,0},{2,3},{3,2},{4,5},{5,4},{6,7},{7,6},{8,9},{9,8},{10,11... | collective-permute-start | bytes 2433032 | tf_op jit(solution)/shard_map/ppermute | solution.py:837
  163.2 46.9 %collective-permute-start.20 = (bf16[528,768]{1,0:T(8,128)(2,1)}, bf16[528,768]{1,0:T(8,128)(2,1)S(1)}, u32[]{:S(2)}, u32[]{:S(2)}) collective-permute-start(bf16[528,768]{1,0:T(8,128)(2,1)} %pad_maximum_fusion.4), channel_id=1, source_target_pairs={{0,2},{1,3},{2,0},{3,1},{4,6},{5,7},{6,4},{7,5},{8,10},{9,11},{10,... | collective-permute-start | bytes 2433032 | tf_op jit(solution)/shard_map/ppermute | solution.py:837
  166.3 43.7 %collective-permute-start.21 = (bf16[528,768]{1,0:T(8,128)(2,1)S(1)}, bf16[528,768]{1,0:T(8,128)(2,1)}, u32[]{:S(2)}, u32[]{:S(2)}) collective-permute-start(bf16[528,768]{1,0:T(8,128)(2,1)S(1)} %pad_maximum_fusion.5), channel_id=1, source_target_pairs={{0,3},{1,2},{2,1},{3,0},{4,7},{5,6},{6,5},{7,4},{8,11},{9,10},{10,... | collective-permute-start | bytes 2433032 | tf_op jit(solution)/shard_map/ppermute | solution.py:837
  212.6 48.9 %collective-permute-start.30 = (bf16[528,768]{1,0:T(8,128)(2,1)S(1)}, bf16[528,768]{1,0:T(8,128)(2,1)S(1)}, u32[]{:S(2)}, u32[]{:S(2)}) collective-permute-start(bf16[528,768]{1,0:T(8,128)(2,1)S(1)} %add_convert_fusion.2), channel_id=1, source_target_pairs={{0,8},{4,12},{24,16},{28,20},{1,9},{5,13},{25,17},{29,21},{2,10},{... | collective-permute-start | bytes 2433032 | tf_op jit(solution)/shard_map/ppermute | solution.py:877
  220.7 40.6 %collective-permute-start.27 = (bf16[96,1152]{1,0:T(8,128)(2,1)S(1)}, bf16[96,1152]{1,0:T(8,128)(2,1)S(1)}, u32[]{:S(2)}, u32[]{:S(2)}) collective-permute-start(bf16[96,1152]{1,0:T(8,128)(2,1)S(1)} %get-tuple-element.151), channel_id=1, source_target_pairs={{0,1},{1,0},{2,3},{3,2},{4,5},{5,4},{6,7},{7,6},{8,9},{9,8},{10,11... | collective-permute-start | bytes 663560 | tf_op jit(solution)/shard_map/ppermute | solution.py:837
  220.8 40.5 %collective-permute-start.28 = (bf16[96,1152]{1,0:T(8,128)(2,1)S(1)}, bf16[96,1152]{1,0:T(8,128)(2,1)S(1)}, u32[]{:S(2)}, u32[]{:S(2)}) collective-permute-start(bf16[96,1152]{1,0:T(8,128)(2,1)S(1)} %get-tuple-element.152), channel_id=1, source_target_pairs={{0,2},{1,3},{2,0},{3,1},{4,6},{5,7},{6,4},{7,5},{8,10},{9,11},{10,... | collective-permute-start | bytes 663560 | tf_op jit(solution)/shard_map/ppermute | solution.py:837
  225.1 36.2 %collective-permute-start.29 = (bf16[96,1152]{1,0:T(8,128)(2,1)S(1)}, bf16[96,1152]{1,0:T(8,128)(2,1)S(1)}, u32[]{:S(2)}, u32[]{:S(2)}) collective-permute-start(bf16[96,1152]{1,0:T(8,128)(2,1)S(1)} %get-tuple-element.153), channel_id=1, source_target_pairs={{0,3},{1,2},{2,1},{3,0},{4,7},{5,6},{6,5},{7,4},{8,11},{9,10},{10,... | collective-permute-start | bytes 663560 | tf_op jit(solution)/shard_map/ppermute | solution.py:837
  261.7 12.1 %collective-permute-start.37 = (bf16[528,768]{1,0:T(8,128)(2,1)S(1)}, bf16[528,768]{1,0:T(8,128)(2,1)S(1)}, u32[]{:S(2)}, u32[]{:S(2)}) collective-permute-start(bf16[528,768]{1,0:T(8,128)(2,1)S(1)} %add_convert_fusion.1), channel_id=1, source_target_pairs={{8,16},{12,20},{16,8},{20,12},{9,17},{13,21},{17,9},{21,13},{10,18... | collective-permute-start | bytes 2433032 | tf_op jit(solution)/shard_map/ppermute | solution.py:881
  278.6 12.7 %collective-permute-start.35 = (bf16[96,1152]{1,0:T(8,128)(2,1)S(1)}, bf16[96,1152]{1,0:T(8,128)(2,1)S(1)}, u32[]{:S(2)}, u32[]{:S(2)}) collective-permute-start(bf16[96,1152]{1,0:T(8,128)(2,1)S(1)} %get-tuple-element.192), channel_id=1, source_target_pairs={{0,2},{1,3},{2,0},{3,1},{4,6},{5,7},{6,4},{7,5},{8,10},{9,11},{10,... | collective-permute-start | bytes 663560 | tf_op jit(solution)/shard_map/ppermute | solution.py:837
  291.5 19.9 %collective-permute-start.39 = (bf16[96,1152]{1,0:T(8,128)(2,1)S(1)}, bf16[96,1152]{1,0:T(8,128)(2,1)S(1)}, u32[]{:S(2)}, u32[]{:S(2)}) collective-permute-start(bf16[96,1152]{1,0:T(8,128)(2,1)S(1)} %convert_element_type.403), channel_id=1, source_target_pairs={{0,8},{4,12},{24,16},{28,20},{1,9},{5,13},{25,17},{29,21},{2,10},{... | collective-permute-start | bytes 663560 | tf_op jit(solution)/shard_map/ppermute | solution.py:877
  307.1 37.9 %collective-permute-start.42 = (bf16[528,768]{1,0:T(8,128)(2,1)S(1)}, bf16[528,768]{1,0:T(8,128)(2,1)S(1)}, u32[]{:S(2)}, u32[]{:S(2)}) collective-permute-start(bf16[528,768]{1,0:T(8,128)(2,1)S(1)} %add_convert_fusion), channel_id=1, source_target_pairs={{8,0},{12,4},{16,24},{20,28},{9,1},{13,5},{17,25},{21,29},{10,2},{... | collective-permute-start | bytes 2433032 | tf_op jit(solution)/shard_map/ppermute | solution.py:885
  308.4 24.6 %collective-permute-start.38 = (bf16[96,1152]{1,0:T(8,128)(2,1)S(1)}, bf16[96,1152]{1,0:T(8,128)(2,1)S(1)}, u32[]{:S(2)}, u32[]{:S(2)}) collective-permute-start(bf16[96,1152]{1,0:T(8,128)(2,1)S(1)} %add_convert_fusion.14), channel_id=1, source_target_pairs={{8,0},{12,4},{16,24},{20,28},{9,1},{13,5},{17,25},{21,29},{10,2},{... | collective-permute-start | bytes 663560 | tf_op jit(solution)/shard_map/ppermute | solution.py:885
  (45 other events, 320.9 us)
